TPU v7x, 512 devices: a whole 4x8x8 slice. The times are simulated.
512 devices in a mesh: shard: 2 (over x_lo), row: 16 (over x_hi, z), col: 16 (over y, core).
Axes of the slice: x: 4 (x_hi: 2, x_lo: 2; x = x_hi * 2 + x_lo), y: 8, z: 8, core: 2. Of those that a mesh axis runs over, the one named last changes fastest.
Arguments:
- params: float32 [16, 16, 16, 5120], P('row', 'col', 'shard'), may hold values from -6 to 6
- public_copy: float32 [16, 16, 16, 5120], P('row', 'col', 'shard'), may hold values from -6 to 6
- neighbour_mix: float32 [16, 16, 16, 5120], P('row', 'col', 'shard'), may hold values from -6 to 6
- row_orders: int32 [2, 5, 1024], replicated, may hold values from 0 to 1023, each once within a row
- sign_bits: int32 [2, 5120], replicated, may hold values from 0 to 1
Outputs:
- new_params: float32 [16, 16, 16, 5120], P('row', 'col', 'shard')
- new_public: float32 [16, 16, 16, 5120], P('row', 'col', 'shard')
- new_mix: float32 [16, 16, 16, 5120], P('row', 'col', 'shard')
Inputs may be any that keep to these rules, and one draw needn't show every extreme that they name: Each row of row_orders is a permutation of 0 to 1023; its first 256 entries are the kept rows.
All inputs are finite; a program needn't handle non-finite values.
Results may differ from a plain program's by a relative error of at most 0.00011.
Values sent between devices are 32-bit elements; how exact they have to be, the bound alone decides.
A program may use at most 64 MiB of HBM per device.

v0:
```python
import jax
import jax.numpy as jnp
from jax import lax
from jax.sharding import PartitionSpec as P

W = 5120
B = 1024
K = 256
ROUNDS = 2


mix_weight = 0.2
step_gamma = 0.5


def shifted(shard, axis, by):
    size = lax.axis_size(axis)
    return lax.ppermute(shard, axis, [(i, (i + by) % size) for i in range(size)])


def projection(orders, bits, keep, block):
    kept = orders[:, :keep]
    column = lax.iota(jnp.int32, block)
    value = jnp.bitwise_and(kept[:, :, None], column[None, None, :])
    value = jnp.bitwise_xor(value, jnp.right_shift(value, 16))
    value = jnp.bitwise_xor(value, jnp.right_shift(value, 8))
    value = jnp.bitwise_xor(value, jnp.right_shift(value, 4))
    value = jnp.bitwise_xor(value, jnp.right_shift(value, 2))
    value = jnp.bitwise_xor(value, jnp.right_shift(value, 1))
    parity = jnp.bitwise_and(value, 1)
    signs = (2 * bits - 1).reshape(orders.shape[0], 1, block)
    entries = (1 - 2 * parity) * signs
    return entries.astype(jnp.float32) / jnp.sqrt(jnp.float32(block))


def encode(diff, proj):
    return jnp.einsum("rjb,jkb->rjk", diff, proj, precision=lax.Precision.HIGHEST)


def decode_pair(stacked, proj):
    rows = stacked.shape[1]
    values = jnp.einsum("srjk,jkb->srjb", stacked, proj, precision=lax.Precision.HIGHEST)
    return (jnp.float32(B / K) * values).reshape(2, rows, W)


def local(params, public_copy, neighbour_mix, row_orders, sign_bits):
    current = params[0, 0]
    public = public_copy[0, 0]
    mixed = neighbour_mix[0, 0]
    rows = current.shape[0]
    blocks = W // B
    for round_index in range(ROUNDS):
        proj = projection(row_orders[round_index], sign_bits[round_index], K, B)
        diff = (current - public).reshape(rows, blocks, B)
        code = encode(diff, proj)
        before_row = shifted(code, "row", 1)
        after_row = shifted(code, "row", -1)
        before_col = shifted(code, "col", 1)
        after_col = shifted(code, "col", -1)
        total = mix_weight * (code + before_row + after_row + before_col + after_col)
        decoded = decode_pair(jnp.stack([code, total]), proj)
        public = public + decoded[0]
        mixed = mixed + decoded[1]
        current = current + step_gamma * (mixed - public)
    return (current[None, None], public[None, None], mixed[None, None])


def solution(mesh):
    placed = (
        P("row", "col", "shard", None),
        P("row", "col", "shard", None),
        P("row", "col", "shard", None),
        P(),
        P(),
    )
    return jax.shard_map(
        local,
        mesh=mesh,
        in_specs=placed,
        out_specs=(
            P("row", "col", "shard", None),
            P("row", "col", "shard", None),
            P("row", "col", "shard", None),
        ),
        check_vma=False,
    )
```

profile of v0, /device:TPU:24, one launch (start us, length us, event | category | flops | bytes accessed | tf_op | source)
XLA Modules:
  0.0 72.3 jit_solution(15067903435175719016)
XLA Ops:
  0.6 0.9 %fusion.110 = (s32[1,5,1024]{2,0,1:T(1,128)S(1)}, s32[1,5,1024]{2,0,1:T(1,128)S(1)}) fusion(s32[2,5,1024]{2,0,1:T(2,128)} %param.8), kind=kLoop, calls=%fused_computation.116 | loop fusion | bytes 81920 | tf_op jit(solution)/shard_map/slice | solution.py:53
  1.6 1.0 %add_reduce_fusion.1 = (s32[5120]{0:T(1024)S(1)}, s32[5120]{0:T(1024)S(1)}) fusion(s32[2,5120]{1,0:T(2,128)} %param.9), kind=kLoop, calls=%fused_computation.86 | loop fusion | flops 20480 | bytes 81920 | tf_op jit(solution)/shard_map/sub | solution.py:31
  2.5 8.4 %fusion.18 = f32[5,256,8]{1,2,0:T(8,128)S(1)} fusion(s32[5,1024]{1,0:T(8,128)S(1)} %sub.37, s32[5,256]{1,0:T(8,128)S(1)} %slice.44, f32[8,5,1024]{2,0,1:T(8,128)} %bitcast.74, f32[8,5,1024]{2,0,1:T(8,128)} %bitcast.76), kind=kOutput, calls=%fused_computation.25 | convolution fusion | flops 148152320 | bytes 394240 | tf_op jit(solution)/shard_map/rjb,jkb->rjk/dot_general | solution.py:37
  11.0 13.4 %collective-permute-start.1 = (f32[8,5,256]{2,0,1:T(8,128)S(1)}, f32[8,5,256]{2,0,1:T(8,128)S(1)}, u32[]{:S(2)}, u32[]{:S(2)}) collective-permute-start(f32[8,5,256]{2,0,1:T(8,128)S(1)} %bitcast.81), channel_id=1, source_target_pairs={{0,240},{16,0},{32,16},{48,32},{64,48},{80,64},{96,80},{112,96},{1... | collective-permute-start | bytes 122888 | tf_op jit(solution)/shard_map/ppermute | solution.py:18
  24.4 0.0 collective-permute-start.2
  24.4 1.9 %collective-permute-start = (f32[8,5,256]{2,0,1:T(8,128)S(1)}, f32[8,5,256]{2,0,1:T(8,128)S(1)}, u32[]{:S(2)}, u32[]{:S(2)}) collective-permute-start(f32[8,5,256]{2,0,1:T(8,128)S(1)} %bitcast.83), channel_id=1, source_target_pairs={{0,16},{16,32},{32,48},{48,64},{64,80},{80,96},{96,112},{112,128},... | collective-permute-start | bytes 122888 | tf_op jit(solution)/shard_map/ppermute | solution.py:18
  26.4 1.7 %collective-permute-start.3 = (f32[8,5,256]{2,0,1:T(8,128)S(1)}, f32[8,5,256]{2,0,1:T(8,128)S(1)}, u32[]{:S(2)}, u32[]{:S(2)}) collective-permute-start(f32[8,5,256]{2,0,1:T(8,128)S(1)} %bitcast.84), channel_id=1, source_target_pairs={{0,15},{1,0},{2,1},{3,2},{4,3},{5,4},{6,5},{7,6},{8,7},{9,8},{10,9... | collective-permute-start | bytes 122888 | tf_op jit(solution)/shard_map/ppermute | solution.py:18
  28.1 0.0 collective-permute-done.1
  28.1 0.0 collective-permute-done.2
  28.1 5.8 %collective-permute-done = f32[8,5,256]{2,0,1:T(8,128)S(1)} collective-permute-done((f32[8,5,256]{2,0,1:T(8,128)S(1)}, f32[8,5,256]{2,0,1:T(8,128)S(1)}, u32[]{:S(2)}, u32[]{:S(2)}) %collective-permute-start) | collective-permute-done | bytes 40992 | tf_op jit(solution)/shard_map/ppermute | solution.py:18
  33.9 0.0 collective-permute-done.3
  34.0 0.0 copy-start
  34.0 0.0 copy-start.1
  34.0 0.0 copy-start.2
  34.0 6.6 %fusion.67 = f32[2,8,5,1024]{3,1,0,2:T(8,128)S(1)} fusion(s32[5,1024]{1,0:T(8,128)S(1)} %sub.37, s32[5,256]{1,0:T(8,128)S(1)} %slice.44, f32[1,8,5,256]{3,1,2,0:T(8,128)S(1)} %multiply_bitcast_fusion.1, f32[1,8,5,256]{3,1,2,0:T(8,128)S(1)} %bitcast.85), kind=kOutput, calls=%fused_computation.63 | convolution fusion | flops 274042880 | bytes 435200
  40.6 0.0 copy-done
  40.6 0.0 copy-done.1
  40.6 0.0 copy-done.2
  40.7 7.7 %fusion.14 = f32[5,256,8]{1,2,0:T(8,128)S(1)} fusion(s32[5,1024]{1,0:T(8,128)S(1)} %sub.42, s32[5,256]{1,0:T(8,128)S(1)} %slice.47, f32[8,5,1024]{2,0,1:T(8,128)S(1)} %bitcast.75, f32[8,5,1024]{2,0,1:T(8,128)S(1)} %bitcast.78, f32[8,5,1024]{2,0,1:T(8,128)S(1)} %bitcast.77, f32[2,8,5,1024]{3,1,0,2:T(8,128)S(1)} %fusion.67), kind=kOutput, calls=%fused_computation.23 | convolution fusion | flops 148357120 | bytes 885760 | tf_op jit(solution)/shard_map/rjb,jkb->rjk/dot_general | solution.py:37
  48.4 3.3 %collective-permute-start.5 = (f32[8,5,256]{2,0,1:T(8,128)S(1)}, f32[8,5,256]{2,0,1:T(8,128)S(1)}, u32[]{:S(2)}, u32[]{:S(2)}) collective-permute-start(f32[8,5,256]{2,0,1:T(8,128)S(1)} %bitcast.86), channel_id=1, source_target_pairs={{0,240},{16,0},{32,16},{48,32},{64,48},{80,64},{96,80},{112,96},{1... | collective-permute-start | bytes 122888 | tf_op jit(solution)/shard_map/ppermute | solution.py:18
  51.6 3.7 %collective-permute-start.6 = (f32[8,5,256]{2,0,1:T(8,128)S(1)}, f32[8,5,256]{2,0,1:T(8,128)S(1)}, u32[]{:S(2)}, u32[]{:S(2)}) collective-permute-start(f32[8,5,256]{2,0,1:T(8,128)S(1)} %bitcast.87), channel_id=1, source_target_pairs={{0,1},{1,2},{2,3},{3,4},{4,5},{5,6},{6,7},{7,8},{8,9},{9,10},{10,1... | collective-permute-start | bytes 122888 | tf_op jit(solution)/shard_map/ppermute | solution.py:18
  55.3 1.9 %collective-permute-start.4 = (f32[8,5,256]{2,0,1:T(8,128)S(1)}, f32[8,5,256]{2,0,1:T(8,128)S(1)}, u32[]{:S(2)}, u32[]{:S(2)}) collective-permute-start(f32[8,5,256]{2,0,1:T(8,128)S(1)} %bitcast.88), channel_id=1, source_target_pairs={{0,16},{16,32},{32,48},{48,64},{64,80},{80,96},{96,112},{112,128},... | collective-permute-start | bytes 122888 | tf_op jit(solution)/shard_map/ppermute | solution.py:18
  57.2 0.0 collective-permute-start.7
  57.3 0.0 collective-permute-done.5
  57.3 0.0 collective-permute-done.6
  57.3 7.5 %collective-permute-done.4 = f32[8,5,256]{2,0,1:T(8,128)S(1)} collective-permute-done((f32[8,5,256]{2,0,1:T(8,128)S(1)}, f32[8,5,256]{2,0,1:T(8,128)S(1)}, u32[]{:S(2)}, u32[]{:S(2)}) %collective-permute-start.4) | collective-permute-done | bytes 40992 | tf_op jit(solution)/shard_map/ppermute | solution.py:18
  64.8 0.0 collective-permute-done.7
  64.8 6.6 %fusion.61 = f32[2,8,5,1024]{3,1,0,2:T(8,128)S(1)} fusion(s32[5,1024]{1,0:T(8,128)S(1)} %sub.42, s32[5,256]{1,0:T(8,128)S(1)} %slice.47, f32[1,8,5,256]{3,1,2,0:T(8,128)S(1)} %multiply_bitcast_fusion, f32[1,8,5,256]{3,1,2,0:T(8,128)S(1)} %bitcast.90), kind=kOutput, calls=%fused_computation.61 | convolution fusion | flops 274042880 | bytes 435200
  71.5 0.8 %multiply_add_fusion = (f32[1,1,8,5120]{3,2,1,0:T(8,128)}, f32[1,1,8,5120]{3,2,1,0:T(8,128)}, f32[1,1,8,5120]{3,2,1,0:T(8,128)}) fusion(f32[1,1,8,5120]{3,2,1,0:T(8,128)S(1)} %copy-done, f32[1,1,8,5120]{3,2,1,0:T(8,128)S(1)} %copy-done.1, f32[1,1,8,5120]{3,2,1,0:T(8,128)S(1)} %bitcast.71, f32[1,1,8,5120]{3,2,1,0:T(8,128)S(1)} %copy-done.2, ...), kind=kLoop, calls=%fused_computation.70 | loop fusion | flops 409600 | bytes 1638400 | tf_op jit(solution)/shard_map/add | solution.py:64
  (10 shorter events, 0.1 us)
Async XLA Ops:
  11.0 17.1 %collective-permute-start.1 = (f32[8,5,256]{2,0,1:T(8,128)S(1)}, f32[8,5,256]{2,0,1:T(8,128)S(1)}, u32[]{:S(2)}, u32[]{:S(2)}) collective-permute-start(f32[8,5,256]{2,0,1:T(8,128)S(1)} %bitcast.81), channel_id=1, source_target_pairs={{0,240},{16,0},{32,16},{48,32},{64,48},{80,64},{96,80},{112,96},{1... | collective-permute-start | bytes 122888 | tf_op jit(solution)/shard_map/ppermute | solution.py:18
  24.4 3.7 %collective-permute-start.2 = (f32[8,5,256]{2,0,1:T(8,128)S(1)}, f32[8,5,256]{2,0,1:T(8,128)S(1)}, u32[]{:S(2)}, u32[]{:S(2)}) collective-permute-start(f32[8,5,256]{2,0,1:T(8,128)S(1)} %bitcast.82), channel_id=1, source_target_pairs={{0,1},{1,2},{2,3},{3,4},{4,5},{5,6},{6,7},{7,8},{8,9},{9,10},{10,1... | collective-permute-start | bytes 122888 | tf_op jit(solution)/shard_map/ppermute | solution.py:18
  24.4 9.5 %collective-permute-start = (f32[8,5,256]{2,0,1:T(8,128)S(1)}, f32[8,5,256]{2,0,1:T(8,128)S(1)}, u32[]{:S(2)}, u32[]{:S(2)}) collective-permute-start(f32[8,5,256]{2,0,1:T(8,128)S(1)} %bitcast.83), channel_id=1, source_target_pairs={{0,16},{16,32},{32,48},{48,64},{64,80},{80,96},{96,112},{112,128},... | collective-permute-start | bytes 122888 | tf_op jit(solution)/shard_map/ppermute | solution.py:18
  26.4 7.6 %collective-permute-start.3 = (f32[8,5,256]{2,0,1:T(8,128)S(1)}, f32[8,5,256]{2,0,1:T(8,128)S(1)}, u32[]{:S(2)}, u32[]{:S(2)}) collective-permute-start(f32[8,5,256]{2,0,1:T(8,128)S(1)} %bitcast.84), channel_id=1, source_target_pairs={{0,15},{1,0},{2,1},{3,2},{4,3},{5,4},{6,5},{7,6},{8,7},{9,8},{10,9... | collective-permute-start | bytes 122888 | tf_op jit(solution)/shard_map/ppermute | solution.py:18
  34.0 6.7 %copy-start = (f32[1,1,8,5120]{3,2,1,0:T(8,128)S(1)}, f32[1,1,8,5120]{3,2,1,0:T(8,128)}, u32[]{:S(2)}) copy-start(f32[1,1,8,5120]{3,2,1,0:T(8,128)} %param.5) | copy-start | bytes 491524
  34.0 6.7 %copy-start.1 = (f32[1,1,8,5120]{3,2,1,0:T(8,128)S(1)}, f32[1,1,8,5120]{3,2,1,0:T(8,128)}, u32[]{:S(2)}) copy-start(f32[1,1,8,5120]{3,2,1,0:T(8,128)} %param.6) | copy-start | bytes 491524
  34.0 6.7 %copy-start.2 = (f32[1,1,8,5120]{3,2,1,0:T(8,128)S(1)}, f32[1,1,8,5120]{3,2,1,0:T(8,128)}, u32[]{:S(2)}) copy-start(f32[1,1,8,5120]{3,2,1,0:T(8,128)} %param.7) | copy-start | bytes 491524
  48.4 8.9 %collective-permute-start.5 = (f32[8,5,256]{2,0,1:T(8,128)S(1)}, f32[8,5,256]{2,0,1:T(8,128)S(1)}, u32[]{:S(2)}, u32[]{:S(2)}) collective-permute-start(f32[8,5,256]{2,0,1:T(8,128)S(1)} %bitcast.86), channel_id=1, source_target_pairs={{0,240},{16,0},{32,16},{48,32},{64,48},{80,64},{96,80},{112,96},{1... | collective-permute-start | bytes 122888 | tf_op jit(solution)/shard_map/ppermute | solution.py:18
  51.6 5.6 %collective-permute-start.6 = (f32[8,5,256]{2,0,1:T(8,128)S(1)}, f32[8,5,256]{2,0,1:T(8,128)S(1)}, u32[]{:S(2)}, u32[]{:S(2)}) collective-permute-start(f32[8,5,256]{2,0,1:T(8,128)S(1)} %bitcast.87), channel_id=1, source_target_pairs={{0,1},{1,2},{2,3},{3,4},{4,5},{5,6},{6,7},{7,8},{8,9},{9,10},{10,1... | collective-permute-start | bytes 122888 | tf_op jit(solution)/shard_map/ppermute | solution.py:18
  55.3 9.5 %collective-permute-start.4 = (f32[8,5,256]{2,0,1:T(8,128)S(1)}, f32[8,5,256]{2,0,1:T(8,128)S(1)}, u32[]{:S(2)}, u32[]{:S(2)}) collective-permute-start(f32[8,5,256]{2,0,1:T(8,128)S(1)} %bitcast.88), channel_id=1, source_target_pairs={{0,16},{16,32},{32,48},{48,64},{64,80},{80,96},{96,112},{112,128},... | collective-permute-start | bytes 122888 | tf_op jit(solution)/shard_map/ppermute | solution.py:18
  57.2 7.6 %collective-permute-start.7 = (f32[8,5,256]{2,0,1:T(8,128)S(1)}, f32[8,5,256]{2,0,1:T(8,128)S(1)}, u32[]{:S(2)}, u32[]{:S(2)}) collective-permute-start(f32[8,5,256]{2,0,1:T(8,128)S(1)} %bitcast.89), channel_id=1, source_target_pairs={{0,15},{1,0},{2,1},{3,2},{4,3},{5,4},{6,5},{7,6},{8,7},{9,8},{10,9... | collective-permute-start | bytes 122888 | tf_op jit(solution)/shard_map/ppermute | solution.py:18
where the time goes:
time: 72.7 us; the launch traced here: 72.3 us
  matrix products  29.4 us (40%)
  starting transfers between devices  25.9 us (36%)
  waiting for transfers between devices  13.3 us (18%)
  other arithmetic  1.84 us (3%)
  local copies, waits for them, and re-layouts  0.99 us (1%)
  between operations  0.83 us (1%)
    ppermute x8, starting transfers between devices, shifted(): lax.ppermute(shard, axis, [(i, (i + by) % size) for i in range(size)])  25.9 us
    dot_general x2, matrix products, encode(): jnp.einsum('rjb,jkb->rjk', diff, proj, precision=lax.Precision.HIGHEST)  16.1 us
    ppermute x8, waiting for transfers between devices, shifted(): lax.ppermute(shard, axis, [(i, (i + by) % size) for i in range(size)])  13.3 us
    unnamed x2, matrix products  13.2 us
  transfers between devices with their start and end apart: 8, of which 2 were waited for; matrix products, arithmetic and copies ran while one was open for 0% of the time, Pallas kernels for 0%

commit v1 on v0

v1 whole, which is shorter than its diff:
```python
import functools

import jax
import jax.numpy as jnp
from jax import lax
from jax.experimental import pallas as pl
from jax.experimental.pallas import tpu as pltpu
from jax.sharding import PartitionSpec as P

W = 5120
B = 1024
K = 256
ROUNDS = 2
NB = W // B
LANES = 128
CHUNKS = B // LANES

mix_weight = 0.2
step_gamma = 0.5
decode_scale = 1.0 / K

GROUPS = ((0, 1), (1, 2), (2, 3), (3, 4), (4, 5))

f32 = jnp.float32
bf16 = jnp.bfloat16


def plus_minus(value, bits):
    shift = bits
    while shift > 1:
        shift = (shift + 1) // 2
        value = value ^ (value >> shift)
    return (1 - 2 * (value & 1)).astype(f32)


def low_matrix(order):
    column = lax.broadcasted_iota(jnp.int32, (LANES, K), 0)
    return plus_minus((order & (LANES - 1)) & column, 8).astype(bf16)


def high_signs(order, rows):
    chunk = lax.broadcasted_iota(jnp.int32, (CHUNKS * rows, K), 0) // rows
    return plus_minus((order >> 7) & chunk, 4)


def halves(value):
    top = value.astype(bf16)
    return top, (value - top.astype(f32)).astype(bf16)


def encode(diff, low, high):
    rows = diff.shape[0]
    stacked = jnp.concatenate([diff[:, c * LANES:(c + 1) * LANES] for c in range(CHUNKS)], axis=0)
    both = jnp.concatenate(halves(stacked), axis=1)
    twice = jnp.concatenate([low, low], axis=0)
    parts = high * jnp.dot(both, twice, preferred_element_type=f32)
    return jnp.sum(parts.reshape(CHUNKS, rows, K), axis=0)


def decode(code, low, high):
    rows = code.shape[0]
    spread = high * jnp.concatenate([code] * CHUNKS, axis=0)
    both = jnp.concatenate(halves(spread), axis=0)
    result = lax.dot_general(both, low, (((1,), (1,)), ((), ())), preferred_element_type=f32)
    result = result[:CHUNKS * rows] + result[CHUNKS * rows:]
    return jnp.concatenate([result[c * rows:(c + 1) * rows] for c in range(CHUNKS)], axis=1)


def kernel(n_row, n_col, x_in, h_in, s_in, order_in, bits_in, x_out, h_out, s_out,
           x_v, h_v, s_v, u_v, order_v, bits_v, low_v, high_v, code_v, got_v,
           in_sem, out_sem, send_sem, recv_sem):
    rows = x_v.shape[0]
    row, col = lax.axis_index("row"), lax.axis_index("col")
    neighbours = (
        {"row": lax.rem(row + 1, n_row)},
        {"row": lax.rem(row + n_row - 1, n_row)},
        {"col": lax.rem(col + 1, n_col)},
        {"col": lax.rem(col + n_col - 1, n_col)},
    )

    loads = [
        pltpu.make_async_copy(order_in.at[:, :, pl.ds(0, K)], order_v, in_sem.at[0]),
        pltpu.make_async_copy(bits_in, bits_v, in_sem.at[1]),
        pltpu.make_async_copy(x_in.at[0, 0], x_v, in_sem.at[2]),
        pltpu.make_async_copy(h_in.at[0, 0], h_v, in_sem.at[3]),
        pltpu.make_async_copy(s_in.at[0, 0], s_v, in_sem.at[4]),
    ]
    for load in loads:
        load.start()

    barrier = pltpu.get_barrier_semaphore()
    for neighbour in neighbours:
        pl.semaphore_signal(barrier, inc=1, device_id=neighbour, device_id_type=pl.DeviceIdType.MESH)

    def build(r):
        for j in range(NB):
            order = order_v[r, j:j + 1, :]
            low_v[r, j] = low_matrix(order)
            high_v[r, j] = high_signs(order, rows)

    def columns(j):
        return slice(j * B, (j + 1) * B)

    def sign(r, j):
        return (2 * bits_v[r:r + 1, columns(j)] - 1).astype(f32)

    copies = {}

    def send(r, g):
        first, last = GROUPS[g]
        part = pl.ds(first, last - first)
        for n, neighbour in enumerate(neighbours):
            copy = pltpu.make_async_remote_copy(
                src_ref=code_v.at[r, part],
                dst_ref=got_v.at[r, n, part],
                send_sem=send_sem.at[r, g, n],
                recv_sem=recv_sem.at[r, g, n],
                device_id=neighbour,
                device_id_type=pl.DeviceIdType.MESH,
            )
            copy.start()
            copies[r, g, n] = copy

    def incoming(r, j):
        total = code_v[r, j] + got_v[r, 0, j] + got_v[r, 1, j] + got_v[r, 2, j] + got_v[r, 3, j]
        return sign(r, j) * decode((mix_weight * decode_scale) * total, low_v[r, j], high_v[r, j])

    def own(r, j):
        return sign(r, j) * decode(decode_scale * code_v[r, j], low_v[r, j], high_v[r, j])

    loads[0].wait()
    build(0)
    for load in loads[1:4]:
        load.wait()
    for g, (first, last) in enumerate(GROUPS):
        for j in range(first, last):
            diff = sign(0, j) * (x_v[:, columns(j)] - h_v[:, columns(j)])
            code_v[0, j] = encode(diff, low_v[0, j], high_v[0, j])
        if g == 0:
            pl.semaphore_wait(barrier, 4)
        send(0, g)

    build(1)
    loads[4].wait()
    for j in range(NB):
        cols = columns(j)
        public = h_v[:, cols] + own(0, j)
        h_v[:, cols] = public
        u_v[:, cols] = x_v[:, cols] + step_gamma * s_v[:, cols] - (1 + step_gamma) * public

    for g, (first, last) in enumerate(GROUPS):
        for n in range(4):
            copies[0, g, n].wait_recv()
        for j in range(first, last):
            cols = columns(j)
            update = incoming(0, j)
            s_v[:, cols] = s_v[:, cols] + update
            diff = sign(1, j) * (u_v[:, cols] + step_gamma * update)
            code_v[1, j] = encode(diff, low_v[1, j], high_v[1, j])
        send(1, g)

    for j in range(NB):
        cols = columns(j)
        before = h_v[:, cols]
        public = before + own(1, j)
        h_v[:, cols] = public
        mixed = s_v[:, cols]
        x_v[:, cols] = x_v[:, cols] + step_gamma * (mixed - before) + step_gamma * (mixed - public)
    stores = [pltpu.make_async_copy(h_v, h_out.at[0, 0], out_sem.at[0])]
    stores[0].start()

    for g, (first, last) in enumerate(GROUPS):
        for n in range(4):
            copies[1, g, n].wait_recv()
        for j in range(first, last):
            cols = columns(j)
            update = incoming(1, j)
            s_v[:, cols] = s_v[:, cols] + update
            x_v[:, cols] = x_v[:, cols] + step_gamma * update
    stores.append(pltpu.make_async_copy(x_v, x_out.at[0, 0], out_sem.at[1]))
    stores.append(pltpu.make_async_copy(s_v, s_out.at[0, 0], out_sem.at[2]))
    for store in stores[1:]:
        store.start()
    for copy in copies.values():
        copy.wait_send()
    for store in stores:
        store.wait()


def local(n_row, n_col, params, public_copy, neighbour_mix, row_orders, sign_bits):
    rows = params.shape[2]
    anywhere = pl.BlockSpec(memory_space=pl.ANY)
    shape = jax.ShapeDtypeStruct(params.shape, f32)
    whole = pltpu.VMEM((rows, W), f32)
    return pl.pallas_call(
        functools.partial(kernel, n_row, n_col),
        out_shape=(shape, shape, shape),
        in_specs=[anywhere] * 5,
        out_specs=(anywhere, anywhere, anywhere),
        scratch_shapes=[
            whole, whole, whole, whole,
            pltpu.VMEM((ROUNDS, NB, K), jnp.int32),
            pltpu.VMEM((ROUNDS, W), jnp.int32),
            pltpu.VMEM((ROUNDS, NB, LANES, K), bf16),
            pltpu.VMEM((ROUNDS, NB, CHUNKS * rows, K), f32),
            pltpu.VMEM((ROUNDS, NB, rows, K), f32),
            pltpu.VMEM((ROUNDS, 4, NB, rows, K), f32),
            pltpu.SemaphoreType.DMA((5,)),
            pltpu.SemaphoreType.DMA((3,)),
            pltpu.SemaphoreType.DMA((ROUNDS, len(GROUPS), 4)),
            pltpu.SemaphoreType.DMA((ROUNDS, len(GROUPS), 4)),
        ],
        compiler_params=pltpu.CompilerParams(
            collective_id=0, has_side_effects=True, vmem_limit_bytes=32 * 1024 * 1024
        ),
    )(params, public_copy, neighbour_mix, row_orders, sign_bits)


def solution(mesh):
    split = P("row", "col", "shard", None)
    return jax.shard_map(
        functools.partial(local, mesh.shape["row"], mesh.shape["col"]),
        mesh=mesh,
        in_specs=(split, split, split, P(), P()),
        out_specs=(split, split, split),
        check_vma=False,
    )
```

time: 72.7 us -> 31.3 us (0.43)
  the two profiles are of different devices: /device:TPU:24 before, /device:TPU:32 now
where the time goes in v1:
time: 31.3 us; the launch traced here: 31.1 us
  Pallas kernels  24.9 us (80%)
  local copies, waits for them, and re-layouts  5.55 us (18%)
  between operations  0.67 us (2%)
    pallas_call x1, Pallas kernels, local(): pl.pallas_call(functools.partial(kernel, n_row, n_col), out_shape=(shape,...  24.9 us
    unnamed x12, local copies, waits for them, and re-layouts  5.55 us

profile of v1, /device:TPU:32, one launch (start us, length us, event | category | flops | bytes accessed | tf_op | source)
XLA Modules:
  0.0 31.1 jit_solution(12720535559187726742)
XLA Ops:
  0.6 0.0 copy-start.3
  0.6 0.8 %copy.8.order_in = s32[2,5,1024]{2,1,0:T(8,128)S(1)} copy(s32[2,5,1024]{2,0,1:T(2,128)} %param.8) | data formatting | bytes 81920 | tf_op args[3]
  1.4 0.0 copy-done.3
  1.5 0.0 copy-start
  1.5 0.9 %copy-done = f32[1,1,8,5120]{3,2,1,0:T(8,128)S(1)} copy-done((f32[1,1,8,5120]{3,2,1,0:T(8,128)S(1)}, f32[1,1,8,5120]{3,2,1,0:T(8,128)}, u32[]{:S(2)}) %copy-start) | copy-done | bytes 163864
  2.4 0.0 copy-start.1
  2.4 0.9 %copy-done.1 = f32[1,1,8,5120]{3,2,1,0:T(8,128)S(1)} copy-done((f32[1,1,8,5120]{3,2,1,0:T(8,128)S(1)}, f32[1,1,8,5120]{3,2,1,0:T(8,128)}, u32[]{:S(2)}) %copy-start.1) | copy-done | bytes 163864
  3.3 0.0 copy-start.2
  3.3 0.9 %copy-done.2 = f32[1,1,8,5120]{3,2,1,0:T(8,128)S(1)} copy-done((f32[1,1,8,5120]{3,2,1,0:T(8,128)S(1)}, f32[1,1,8,5120]{3,2,1,0:T(8,128)}, u32[]{:S(2)}) %copy-start.2) | copy-done | bytes 163864
  4.2 24.9 %shard_map.76 = (f32[1,1,8,5120]{3,2,1,0:T(8,128)S(1)}, f32[1,1,8,5120]{3,2,1,0:T(8,128)S(1)}, f32[1,1,8,5120]{3,2,1,0:T(8,128)S(1)}) custom-call(f32[1,1,8,5120]{3,2,1,0:T(8,128)S(1)} %copy-done, f32[1,1,8,5120]{3,2,1,0:T(8,128)S(1)} %copy-done.1, f32[1,1,8,5120]{3,2,1,0:T(8,128)S(1)} %copy-done.2, s32[2,5,1024]{2,1,0:T(8,128)S(1)} %copy.8.order_in, ...), custom_call_target="tpu_custom_call" | custom-call | tf_op jit(solution)/shard_map/pallas_call | solution.py:195
  29.1 0.7 %copy.12 = f32[1,1,8,5120]{3,2,1,0:T(8,128)} copy(f32[1,1,8,5120]{3,2,1,0:T(8,128)S(1)} %get-tuple-element.6) | data formatting | bytes 327680
  29.8 0.7 %copy.13 = f32[1,1,8,5120]{3,2,1,0:T(8,128)} copy(f32[1,1,8,5120]{3,2,1,0:T(8,128)S(1)} %get-tuple-element.7) | data formatting | bytes 327680
  30.4 0.7 %copy.14 = f32[1,1,8,5120]{3,2,1,0:T(8,128)} copy(f32[1,1,8,5120]{3,2,1,0:T(8,128)S(1)} %get-tuple-element.8) | data formatting | bytes 327680
Async XLA Ops:
  0.6 0.8 %copy-start.3 = (s32[2,5120]{1,0:T(2,128)S(1)}, s32[2,5120]{1,0:T(2,128)}, u32[]{:S(2)}) copy-start(s32[2,5120]{1,0:T(2,128)} %bits_in.1) | copy-start | bytes 122884
  1.5 0.9 %copy-start = (f32[1,1,8,5120]{3,2,1,0:T(8,128)S(1)}, f32[1,1,8,5120]{3,2,1,0:T(8,128)}, u32[]{:S(2)}) copy-start(f32[1,1,8,5120]{3,2,1,0:T(8,128)} %x_in.1) | copy-start | bytes 491524
  2.4 0.9 %copy-start.1 = (f32[1,1,8,5120]{3,2,1,0:T(8,128)S(1)}, f32[1,1,8,5120]{3,2,1,0:T(8,128)}, u32[]{:S(2)}) copy-start(f32[1,1,8,5120]{3,2,1,0:T(8,128)} %h_in.1) | copy-start | bytes 491524
  3.3 0.9 %copy-start.2 = (f32[1,1,8,5120]{3,2,1,0:T(8,128)S(1)}, f32[1,1,8,5120]{3,2,1,0:T(8,128)}, u32[]{:S(2)}) copy-start(f32[1,1,8,5120]{3,2,1,0:T(8,128)} %s_in.1) | copy-start | bytes 491524

commit v2 on v1

--- a/solution.py
+++ b/solution.py
@@ -19,7 +19,7 @@
 step_gamma = 0.5
 decode_scale = 1.0 / K
 
-GROUPS = ((0, 1), (1, 2), (2, 3), (3, 4), (4, 5))
+GROUPS = ((0, 5),)
 
 f32 = jnp.float32
 bf16 = jnp.bfloat16
@@ -66,9 +66,9 @@
     return jnp.concatenate([result[c * rows:(c + 1) * rows] for c in range(CHUNKS)], axis=1)
 
 
-def kernel(n_row, n_col, x_in, h_in, s_in, order_in, bits_in, x_out, h_out, s_out,
-           x_v, h_v, s_v, u_v, order_v, bits_v, low_v, high_v, code_v, got_v,
-           in_sem, out_sem, send_sem, recv_sem):
+def kernel(n_row, n_col, x_in, h_in, s_in, order_in, bits_in, x_v, h_v, s_v,
+           u_v, order_v, bits_v, low_v, high_v, code_v, got_v,
+           in_sem, send_sem, recv_sem):
     rows = x_v.shape[0]
     row, col = lax.axis_index("row"), lax.axis_index("col")
     neighbours = (
@@ -94,7 +94,7 @@
 
     def build(r):
         for j in range(NB):
-            order = order_v[r, j:j + 1, :]
+            order = order_v[j, r:r + 1, :]
             low_v[r, j] = low_matrix(order)
             high_v[r, j] = high_signs(order, rows)
 
@@ -166,8 +166,6 @@
         h_v[:, cols] = public
         mixed = s_v[:, cols]
         x_v[:, cols] = x_v[:, cols] + step_gamma * (mixed - before) + step_gamma * (mixed - public)
-    stores = [pltpu.make_async_copy(h_v, h_out.at[0, 0], out_sem.at[0])]
-    stores[0].start()
 
     for g, (first, last) in enumerate(GROUPS):
         for n in range(4):
@@ -177,43 +175,55 @@
             update = incoming(1, j)
             s_v[:, cols] = s_v[:, cols] + update
             x_v[:, cols] = x_v[:, cols] + step_gamma * update
-    stores.append(pltpu.make_async_copy(x_v, x_out.at[0, 0], out_sem.at[1]))
-    stores.append(pltpu.make_async_copy(s_v, s_out.at[0, 0], out_sem.at[2]))
-    for store in stores[1:]:
-        store.start()
     for copy in copies.values():
         copy.wait_send()
-    for store in stores:
-        store.wait()
+
+
+def store_kernel(x_in, h_in, s_in, x_out, h_out, s_out, sem):
+    pairs = ((x_in, x_out), (h_in, h_out), (s_in, s_out))
+    copies = [pltpu.make_async_copy(a, b.at[0, 0], sem.at[i]) for i, (a, b) in enumerate(pairs)]
+    for copy in copies:
+        copy.start()
+    for copy in copies:
+        copy.wait()
 
 
 def local(n_row, n_col, params, public_copy, neighbour_mix, row_orders, sign_bits):
     rows = params.shape[2]
-    anywhere = pl.BlockSpec(memory_space=pl.ANY)
+    hbm = pl.BlockSpec(memory_space=pltpu.HBM)
+    vmem = pl.BlockSpec(memory_space=pltpu.VMEM)
     shape = jax.ShapeDtypeStruct(params.shape, f32)
+    flat = pltpu.VMEM((rows, W), f32)
     whole = pltpu.VMEM((rows, W), f32)
-    return pl.pallas_call(
+    results = pl.pallas_call(
         functools.partial(kernel, n_row, n_col),
-        out_shape=(shape, shape, shape),
-        in_specs=[anywhere] * 5,
-        out_specs=(anywhere, anywhere, anywhere),
+        out_shape=(flat, flat, flat),
+        in_specs=[hbm] * 5,
+        out_specs=(vmem, vmem, vmem),
         scratch_shapes=[
-            whole, whole, whole, whole,
-            pltpu.VMEM((ROUNDS, NB, K), jnp.int32),
+            whole,
+            pltpu.VMEM((NB, ROUNDS, K), jnp.int32),
             pltpu.VMEM((ROUNDS, W), jnp.int32),
             pltpu.VMEM((ROUNDS, NB, LANES, K), bf16),
             pltpu.VMEM((ROUNDS, NB, CHUNKS * rows, K), f32),
             pltpu.VMEM((ROUNDS, NB, rows, K), f32),
             pltpu.VMEM((ROUNDS, 4, NB, rows, K), f32),
             pltpu.SemaphoreType.DMA((5,)),
-            pltpu.SemaphoreType.DMA((3,)),
             pltpu.SemaphoreType.DMA((ROUNDS, len(GROUPS), 4)),
             pltpu.SemaphoreType.DMA((ROUNDS, len(GROUPS), 4)),
         ],
         compiler_params=pltpu.CompilerParams(
             collective_id=0, has_side_effects=True, vmem_limit_bytes=32 * 1024 * 1024
         ),
-    )(params, public_copy, neighbour_mix, row_orders, sign_bits)
+    )(*(pltpu.with_memory_space_constraint(a, pltpu.HBM) for a in (
+        params, public_copy, neighbour_mix, jnp.transpose(row_orders, (1, 0, 2)), sign_bits)))
+    return pl.pallas_call(
+        store_kernel,
+        out_shape=(shape, shape, shape),
+        in_specs=[vmem] * 3,
+        out_specs=(hbm, hbm, hbm),
+        scratch_shapes=[pltpu.SemaphoreType.DMA((3,))],
+    )(*(pltpu.with_memory_space_constraint(a, pltpu.VMEM) for a in results))
 
 
 def solution(mesh):

time: 31.3 us -> 24.3 us (0.78)
  the two profiles are of different devices: /device:TPU:32 before, /device:TPU:40 now
where the time goes in v2:
time: 24.3 us; the launch traced here: 24.2 us
  Pallas kernels  23.5 us (97%)
  between operations  0.64 us (3%)
    pallas_call x1, Pallas kernels, local(): pl.pallas_call(functools.partial(kernel, n_row, n_col), out_shape=(flat,...  22.7 us
    pallas_call x1, Pallas kernels, local(): pl.pallas_call(store_kernel, out_shape=(shape, shape, shape), in_specs=[v...  0.8 us

profile of v2, /device:TPU:40, one launch (start us, length us, event | category | flops | bytes accessed | tf_op | source)
XLA Modules:
  0.0 24.2 jit_solution(15530899916929502686)
XLA Ops:
  0.6 22.7 %shard_map.76 = (f32[8,5120]{1,0:T(8,128)S(1)}, f32[8,5120]{1,0:T(8,128)S(1)}, f32[8,5120]{1,0:T(8,128)S(1)}) custom-call(f32[1,1,8,5120]{3,2,1,0:T(8,128)} %x_in.1, f32[1,1,8,5120]{3,2,1,0:T(8,128)} %h_in.1, f32[1,1,8,5120]{3,2,1,0:T(8,128)} %s_in.1, s32[5,2,1024]{2,1,0:T(2,128)} %bitcast.1, s32[2,5120]{1,0:T(2,128)} %bits_in.1), custom_call_target="tpu_custom_call" | custom-call | tf_op jit(solution)/shard_map/pallas_call | solution.py:198
  23.4 0.8 %shard_map.77 = (f32[1,1,8,5120]{3,2,1,0:T(8,128)}, f32[1,1,8,5120]{3,2,1,0:T(8,128)}, f32[1,1,8,5120]{3,2,1,0:T(8,128)}) custom-call(f32[8,5120]{1,0:T(8,128)S(1)} %get-tuple-element.6.x_in, f32[8,5120]{1,0:T(8,128)S(1)} %get-tuple-element.7.h_in, f32[8,5120]{1,0:T(8,128)S(1)} %get-tuple-element.8.s_in), custom_call_target="tpu_custom_call" | custom-call | tf_op jit(solution)/shard_map/pallas_call | solution.py:220

commit v3 on v2

--- a/solution.py
+++ b/solution.py
@@ -19,7 +19,8 @@
 step_gamma = 0.5
 decode_scale = 1.0 / K
 
-GROUPS = ((0, 5),)
+EDGE = 8
+NEXT_ROW, PREV_ROW, NEXT_COL, PREV_COL = range(4)
 
 f32 = jnp.float32
 bf16 = jnp.bfloat16
@@ -67,7 +68,7 @@
 
 
 def kernel(n_row, n_col, x_in, h_in, s_in, order_in, bits_in, x_v, h_v, s_v,
-           u_v, order_v, bits_v, low_v, high_v, code_v, got_v,
+           order_v, bits_v, low_v, high_v, code_v, first_v, self_v, got_v,
            in_sem, send_sem, recv_sem):
     rows = x_v.shape[0]
     row, col = lax.axis_index("row"), lax.axis_index("col")
@@ -85,12 +86,11 @@
         pltpu.make_async_copy(h_in.at[0, 0], h_v, in_sem.at[3]),
         pltpu.make_async_copy(s_in.at[0, 0], s_v, in_sem.at[4]),
     ]
-    for load in loads:
-        load.start()
-
     barrier = pltpu.get_barrier_semaphore()
     for neighbour in neighbours:
         pl.semaphore_signal(barrier, inc=1, device_id=neighbour, device_id_type=pl.DeviceIdType.MESH)
+    for load in loads:
+        load.start()
 
     def build(r):
         for j in range(NB):
@@ -104,79 +104,100 @@
     def sign(r, j):
         return (2 * bits_v[r:r + 1, columns(j)] - 1).astype(f32)
 
-    copies = {}
-
-    def send(r, g):
-        first, last = GROUPS[g]
-        part = pl.ds(first, last - first)
-        for n, neighbour in enumerate(neighbours):
-            copy = pltpu.make_async_remote_copy(
-                src_ref=code_v.at[r, part],
-                dst_ref=got_v.at[r, n, part],
-                send_sem=send_sem.at[r, g, n],
-                recv_sem=recv_sem.at[r, g, n],
-                device_id=neighbour,
-                device_id_type=pl.DeviceIdType.MESH,
-            )
-            copy.start()
-            copies[r, g, n] = copy
-
-    def incoming(r, j):
-        total = code_v[r, j] + got_v[r, 0, j] + got_v[r, 1, j] + got_v[r, 2, j] + got_v[r, 3, j]
-        return sign(r, j) * decode((mix_weight * decode_scale) * total, low_v[r, j], high_v[r, j])
-
-    def own(r, j):
-        return sign(r, j) * decode(decode_scale * code_v[r, j], low_v[r, j], high_v[r, j])
+    def copy(r, n, source):
+        return pltpu.make_async_remote_copy(
+            src_ref=source,
+            dst_ref=got_v.at[r, n],
+            send_sem=send_sem.at[r, n],
+            recv_sem=recv_sem.at[r, n],
+            device_id=neighbours[n],
+            device_id_type=pl.DeviceIdType.MESH,
+        )
+
+    def send(r, targets, source):
+        for n in targets:
+            copy(r, n, source).start()
+
+    def receive(r, sources):
+        for n in sources:
+            pltpu.make_async_copy(got_v.at[r, n], got_v.at[r, n], recv_sem.at[r, n]).wait()
+
+    def spread(r, j, code):
+        return sign(r, j) * decode(decode_scale * code, low_v[r, j], high_v[r, j])
+
+    def later(j, update):
+        return encode(sign(1, j) * update, low_v[1, j], high_v[1, j])
 
     loads[0].wait()
     build(0)
     for load in loads[1:4]:
         load.wait()
-    for g, (first, last) in enumerate(GROUPS):
-        for j in range(first, last):
-            diff = sign(0, j) * (x_v[:, columns(j)] - h_v[:, columns(j)])
-            code_v[0, j] = encode(diff, low_v[0, j], high_v[0, j])
-        if g == 0:
-            pl.semaphore_wait(barrier, 4)
-        send(0, g)
+    for j in range(NB):
+        cols = columns(j)
+        code_v[0, j] = encode(sign(0, j) * (x_v[:, cols] - h_v[:, cols]), low_v[0, j], high_v[0, j])
+    pl.semaphore_wait(barrier, 4)
+    send(0, (NEXT_COL, PREV_COL, NEXT_ROW, PREV_ROW), code_v.at[0])
 
     build(1)
     loads[4].wait()
     for j in range(NB):
         cols = columns(j)
-        public = h_v[:, cols] + own(0, j)
+        update = spread(0, j, code_v[0, j])
+        public = h_v[:, cols] + update
+        share = mix_weight * update
+        mixed = s_v[:, cols]
+        x_v[:, cols] = x_v[:, cols] - step_gamma * public
+        base = x_v[:, cols] + step_gamma * mixed - public
         h_v[:, cols] = public
-        u_v[:, cols] = x_v[:, cols] + step_gamma * s_v[:, cols] - (1 + step_gamma) * public
-
-    for g, (first, last) in enumerate(GROUPS):
+        s_v[:, cols] = mixed + share
+        self_v[j] = later(j, step_gamma * share)
+        first_v[j] = later(j, base) + self_v[j]
+
+    edge = lax.rem(row, EDGE) == 0
+    early = jnp.where(edge, PREV_ROW, NEXT_ROW)
+    late = jnp.where(edge, NEXT_ROW, PREV_ROW)
+    receive(0, (early, NEXT_COL, PREV_COL))
+    for j in range(NB):
+        cols = columns(j)
+        update = spread(0, j, mix_weight * (got_v[0, early, j] + got_v[0, NEXT_COL, j] + got_v[0, PREV_COL, j]))
+        s_v[:, cols] = s_v[:, cols] + update
+        first_v[j] = first_v[j] + later(j, step_gamma * update)
+
+    @pl.when(jnp.logical_not(edge))
+    def _():
+        send(1, (NEXT_ROW,), first_v)
+
+    receive(0, (late,))
+    for j in range(NB):
+        cols = columns(j)
+        update = spread(0, j, mix_weight * got_v[0, late, j])
+        s_v[:, cols] = s_v[:, cols] + update
+        code_v[1, j] = first_v[j] + later(j, step_gamma * update)
+    send(1, (NEXT_COL, PREV_COL, PREV_ROW), code_v.at[1])
+
+    @pl.when(edge)
+    def _():
+        send(1, (NEXT_ROW,), code_v.at[1])
+
+    for j in range(NB):
+        cols = columns(j)
+        public = h_v[:, cols] + spread(1, j, code_v[1, j])
+        h_v[:, cols] = public
+        x_v[:, cols] = x_v[:, cols] + step_gamma * (2 * s_v[:, cols] - public)
+
+    left_out = jnp.where(lax.rem(row, EDGE) == 1, 0.0, 1.0)
+    receive(1, range(4))
+    for j in range(NB):
+        cols = columns(j)
+        total = code_v[1, j] + left_out * self_v[j]
         for n in range(4):
-            copies[0, g, n].wait_recv()
-        for j in range(first, last):
-            cols = columns(j)
-            update = incoming(0, j)
-            s_v[:, cols] = s_v[:, cols] + update
-            diff = sign(1, j) * (u_v[:, cols] + step_gamma * update)
-            code_v[1, j] = encode(diff, low_v[1, j], high_v[1, j])
-        send(1, g)
-
-    for j in range(NB):
-        cols = columns(j)
-        before = h_v[:, cols]
-        public = before + own(1, j)
-        h_v[:, cols] = public
-        mixed = s_v[:, cols]
-        x_v[:, cols] = x_v[:, cols] + step_gamma * (mixed - before) + step_gamma * (mixed - public)
-
-    for g, (first, last) in enumerate(GROUPS):
+            total = total + got_v[1, n, j]
+        update = spread(1, j, mix_weight * total)
+        s_v[:, cols] = s_v[:, cols] + update
+        x_v[:, cols] = x_v[:, cols] + step_gamma * update
+    for r in range(ROUNDS):
         for n in range(4):
-            copies[1, g, n].wait_recv()
-        for j in range(first, last):
-            cols = columns(j)
-            update = incoming(1, j)
-            s_v[:, cols] = s_v[:, cols] + update
-            x_v[:, cols] = x_v[:, cols] + step_gamma * update
-    for copy in copies.values():
-        copy.wait_send()
+            copy(r, n, code_v.at[r]).wait_send()
 
 
 def store_kernel(x_in, h_in, s_in, x_out, h_out, s_out, sem):
@@ -194,23 +215,23 @@
     vmem = pl.BlockSpec(memory_space=pltpu.VMEM)
     shape = jax.ShapeDtypeStruct(params.shape, f32)
     flat = pltpu.VMEM((rows, W), f32)
-    whole = pltpu.VMEM((rows, W), f32)
     results = pl.pallas_call(
         functools.partial(kernel, n_row, n_col),
         out_shape=(flat, flat, flat),
         in_specs=[hbm] * 5,
         out_specs=(vmem, vmem, vmem),
         scratch_shapes=[
-            whole,
             pltpu.VMEM((NB, ROUNDS, K), jnp.int32),
             pltpu.VMEM((ROUNDS, W), jnp.int32),
             pltpu.VMEM((ROUNDS, NB, LANES, K), bf16),
             pltpu.VMEM((ROUNDS, NB, CHUNKS * rows, K), f32),
             pltpu.VMEM((ROUNDS, NB, rows, K), f32),
+            pltpu.VMEM((NB, rows, K), f32),
+            pltpu.VMEM((NB, rows, K), f32),
             pltpu.VMEM((ROUNDS, 4, NB, rows, K), f32),
             pltpu.SemaphoreType.DMA((5,)),
-            pltpu.SemaphoreType.DMA((ROUNDS, len(GROUPS), 4)),
-            pltpu.SemaphoreType.DMA((ROUNDS, len(GROUPS), 4)),
+            pltpu.SemaphoreType.DMA((ROUNDS, 4)),
+            pltpu.SemaphoreType.DMA((ROUNDS, 4)),
         ],
         compiler_params=pltpu.CompilerParams(
             collective_id=0, has_side_effects=True, vmem_limit_bytes=32 * 1024 * 1024

time: 24.3 us -> 22.8 us (0.938)
  the two profiles are of different devices: /device:TPU:40 before, /device:TPU:1 now
where the time goes in v3:
time: 22.8 us; the launch traced here: 22.7 us
  Pallas kernels  22 us (96%)
  between operations  0.64 us (3%)
    pallas_call x1, Pallas kernels, local(): pl.pallas_call(functools.partial(kernel, n_row, n_col), out_shape=(flat,...  21.2 us
    pallas_call x1, Pallas kernels, local(): pl.pallas_call(store_kernel, out_shape=(shape, shape, shape), in_specs=[v...  0.8 us

profile of v3, /device:TPU:1, one launch (start us, length us, event | category | flops | bytes accessed | tf_op | source)
XLA Modules:
  0.0 22.7 jit_solution(2087407288922737361)
XLA Ops:
  0.6 21.2 %shard_map.76 = (f32[8,5120]{1,0:T(8,128)S(1)}, f32[8,5120]{1,0:T(8,128)S(1)}, f32[8,5120]{1,0:T(8,128)S(1)}) custom-call(f32[1,1,8,5120]{3,2,1,0:T(8,128)} %x_in.1, f32[1,1,8,5120]{3,2,1,0:T(8,128)} %h_in.1, f32[1,1,8,5120]{3,2,1,0:T(8,128)} %s_in.1, s32[5,2,1024]{2,1,0:T(2,128)} %bitcast.1, s32[2,5120]{1,0:T(2,128)} %bits_in.1), custom_call_target="tpu_custom_call" | custom-call | tf_op jit(solution)/shard_map/pallas_call | solution.py:218
  21.9 0.8 %shard_map.77 = (f32[1,1,8,5120]{3,2,1,0:T(8,128)}, f32[1,1,8,5120]{3,2,1,0:T(8,128)}, f32[1,1,8,5120]{3,2,1,0:T(8,128)}) custom-call(f32[8,5120]{1,0:T(8,128)S(1)} %get-tuple-element.6.x_in, f32[8,5120]{1,0:T(8,128)S(1)} %get-tuple-element.7.h_in, f32[8,5120]{1,0:T(8,128)S(1)} %get-tuple-element.8.s_in), custom_call_target="tpu_custom_call" | custom-call | tf_op jit(solution)/shard_map/pallas_call | solution.py:241

commit v4 on v3

--- a/solution.py
+++ b/solution.py
@@ -68,7 +68,8 @@
 
 
 def kernel(n_row, n_col, x_in, h_in, s_in, order_in, bits_in, x_v, h_v, s_v,
-           order_v, bits_v, low_v, high_v, code_v, first_v, self_v, got_v,
+           order_v, bits_v, low_v, high_v, code_v, got_v,
+           self_v, base_v, rows_v, cols_v, next_v, last_v, side_v, both_v, full_v,
            in_sem, send_sem, recv_sem):
     rows = x_v.shape[0]
     row, col = lax.axis_index("row"), lax.axis_index("col")
@@ -86,9 +87,23 @@
         pltpu.make_async_copy(h_in.at[0, 0], h_v, in_sem.at[3]),
         pltpu.make_async_copy(s_in.at[0, 0], s_v, in_sem.at[4]),
     ]
+    edge = lax.rem(row, EDGE) == 0
+    inner = jnp.logical_not(edge)
+    before_edge = lax.rem(row, EDGE) == EDGE - 1
+    even = lax.rem(col, 2) == 0
+    odd = jnp.logical_not(even)
+    early = jnp.where(edge, PREV_ROW, NEXT_ROW)
+    late = jnp.where(edge, NEXT_ROW, PREV_ROW)
+
     barrier = pltpu.get_barrier_semaphore()
-    for neighbour in neighbours:
-        pl.semaphore_signal(barrier, inc=1, device_id=neighbour, device_id_type=pl.DeviceIdType.MESH)
+
+    def greet(n):
+        pl.semaphore_signal(barrier, inc=1, device_id=neighbours[n], device_id_type=pl.DeviceIdType.MESH)
+
+    greet(NEXT_COL)
+    greet(PREV_COL)
+    greet(PREV_ROW)
+    pl.when(jnp.logical_not(before_edge))(lambda: greet(NEXT_ROW))
     for load in loads:
         load.start()
 
@@ -135,8 +150,9 @@
     for j in range(NB):
         cols = columns(j)
         code_v[0, j] = encode(sign(0, j) * (x_v[:, cols] - h_v[:, cols]), low_v[0, j], high_v[0, j])
-    pl.semaphore_wait(barrier, 4)
-    send(0, (NEXT_COL, PREV_COL, NEXT_ROW, PREV_ROW), code_v.at[0])
+    pl.semaphore_wait(barrier, jnp.where(edge, 3, 4))
+    send(0, (NEXT_COL, PREV_COL, NEXT_ROW), code_v.at[0])
+    pl.when(inner)(lambda: send(0, (PREV_ROW,), code_v.at[0]))
 
     build(1)
     loads[4].wait()
@@ -151,37 +167,46 @@
         h_v[:, cols] = public
         s_v[:, cols] = mixed + share
         self_v[j] = later(j, step_gamma * share)
-        first_v[j] = later(j, base) + self_v[j]
-
-    edge = lax.rem(row, EDGE) == 0
-    early = jnp.where(edge, PREV_ROW, NEXT_ROW)
-    late = jnp.where(edge, NEXT_ROW, PREV_ROW)
-    receive(0, (early, NEXT_COL, PREV_COL))
-    for j in range(NB):
-        cols = columns(j)
-        update = spread(0, j, mix_weight * (got_v[0, early, j] + got_v[0, NEXT_COL, j] + got_v[0, PREV_COL, j]))
+        base_v[j] = later(j, base) + self_v[j]
+
+    twice = jnp.where(even, 0.0, 2.0)
+
+    def part(j, code):
+        cols = columns(j)
+        update = spread(0, j, mix_weight * code)
         s_v[:, cols] = s_v[:, cols] + update
-        first_v[j] = first_v[j] + later(j, step_gamma * update)
-
-    @pl.when(jnp.logical_not(edge))
-    def _():
-        send(1, (NEXT_ROW,), first_v)
+        return later(j, step_gamma * update)
+
+    receive(0, (early,))
+    for j in range(NB):
+        rows_v[j] = part(j, got_v[0, early, j])
+        next_v[j] = base_v[j] + rows_v[j]
+    pl.when(jnp.logical_and(inner, even))(lambda: send(1, (NEXT_ROW,), next_v))
+
+    receive(0, (NEXT_COL, PREV_COL))
+    for j in range(NB):
+        cols_v[j] = part(j, got_v[0, NEXT_COL, j] + got_v[0, PREV_COL, j])
+        last_v[j] = base_v[j] + rows_v[j] + twice * cols_v[j]
+        side_v[j] = base_v[j] + cols_v[j]
+    pl.when(jnp.logical_and(inner, odd))(lambda: send(1, (NEXT_ROW,), last_v))
+    pl.when(even)(lambda: send(1, (NEXT_COL, PREV_COL), side_v))
 
     receive(0, (late,))
-    for j in range(NB):
-        cols = columns(j)
-        update = spread(0, j, mix_weight * got_v[0, late, j])
-        s_v[:, cols] = s_v[:, cols] + update
-        code_v[1, j] = first_v[j] + later(j, step_gamma * update)
-    send(1, (NEXT_COL, PREV_COL, PREV_ROW), code_v.at[1])
-
-    @pl.when(edge)
-    def _():
-        send(1, (NEXT_ROW,), code_v.at[1])
-
-    for j in range(NB):
-        cols = columns(j)
-        public = h_v[:, cols] + spread(1, j, code_v[1, j])
+    pl.when(edge)(lambda: send(0, (PREV_ROW,), code_v.at[0]))
+    for j in range(NB):
+        late_part = part(j, got_v[0, late, j])
+        rows_v[j] = rows_v[j] + late_part
+        code_v[1, j] = last_v[j] + late_part
+        both_v[j] = side_v[j] + twice * rows_v[j]
+    pl.when(odd)(lambda: send(1, (NEXT_COL, PREV_COL), both_v))
+    pl.when(edge)(lambda: send(1, (NEXT_ROW,), code_v.at[1]))
+    send(1, (PREV_ROW,), code_v.at[1])
+
+    for j in range(NB):
+        cols = columns(j)
+        own = base_v[j] + rows_v[j] + cols_v[j]
+        full_v[j] = own
+        public = h_v[:, cols] + spread(1, j, own)
         h_v[:, cols] = public
         x_v[:, cols] = x_v[:, cols] + step_gamma * (2 * s_v[:, cols] - public)
 
@@ -189,7 +214,7 @@
     receive(1, range(4))
     for j in range(NB):
         cols = columns(j)
-        total = code_v[1, j] + left_out * self_v[j]
+        total = full_v[j] + left_out * self_v[j]
         for n in range(4):
             total = total + got_v[1, n, j]
         update = spread(1, j, mix_weight * total)
@@ -226,9 +251,8 @@
             pltpu.VMEM((ROUNDS, NB, LANES, K), bf16),
             pltpu.VMEM((ROUNDS, NB, CHUNKS * rows, K), f32),
             pltpu.VMEM((ROUNDS, NB, rows, K), f32),
-            pltpu.VMEM((NB, rows, K), f32),
-            pltpu.VMEM((NB, rows, K), f32),
             pltpu.VMEM((ROUNDS, 4, NB, rows, K), f32),
+        ] + [pltpu.VMEM((NB, rows, K), f32)] * 9 + [
             pltpu.SemaphoreType.DMA((5,)),
             pltpu.SemaphoreType.DMA((ROUNDS, 4)),
             pltpu.SemaphoreType.DMA((ROUNDS, 4)),

time: 22.8 us -> 21.9 us (0.961)
  the two profiles are of different devices: /device:TPU:1 before, /device:TPU:25 now
where the time goes in v4:
time: 21.9 us; the launch traced here: 21.8 us
  Pallas kernels  21.1 us (96%)
  between operations  0.64 us (3%)
    pallas_call x1, Pallas kernels, local(): pl.pallas_call(functools.partial(kernel, n_row, n_col), out_shape=(flat,...  20.3 us
    pallas_call x1, Pallas kernels, local(): pl.pallas_call(store_kernel, out_shape=(shape, shape, shape), in_specs=[v...  0.8 us

profile of v4, /device:TPU:25, one launch (start us, length us, event | category | flops | bytes accessed | tf_op | source)
XLA Modules:
  0.0 21.8 jit_solution(8669000625609026111)
XLA Ops:
  0.6 20.3 %shard_map.76 = (f32[8,5120]{1,0:T(8,128)S(1)}, f32[8,5120]{1,0:T(8,128)S(1)}, f32[8,5120]{1,0:T(8,128)S(1)}) custom-call(f32[1,1,8,5120]{3,2,1,0:T(8,128)} %x_in.1, f32[1,1,8,5120]{3,2,1,0:T(8,128)} %h_in.1, f32[1,1,8,5120]{3,2,1,0:T(8,128)} %s_in.1, s32[5,2,1024]{2,1,0:T(2,128)} %bitcast.1, s32[2,5120]{1,0:T(2,128)} %bits_in.1), custom_call_target="tpu_custom_call" | custom-call | tf_op jit(solution)/shard_map/pallas_call | solution.py:243
  21.0 0.8 %shard_map.77 = (f32[1,1,8,5120]{3,2,1,0:T(8,128)}, f32[1,1,8,5120]{3,2,1,0:T(8,128)}, f32[1,1,8,5120]{3,2,1,0:T(8,128)}) custom-call(f32[8,5120]{1,0:T(8,128)S(1)} %get-tuple-element.6.x_in, f32[8,5120]{1,0:T(8,128)S(1)} %get-tuple-element.7.h_in, f32[8,5120]{1,0:T(8,128)S(1)} %get-tuple-element.8.s_in), custom_call_target="tpu_custom_call" | custom-call | tf_op jit(solution)/shard_map/pallas_call | solution.py:265

commit v5 on v4

v5 whole, which is shorter than its diff:
```python
import functools

import jax
import jax.numpy as jnp
from jax import lax
from jax.experimental import pallas as pl
from jax.experimental.pallas import tpu as pltpu
from jax.sharding import PartitionSpec as P

W = 5120
B = 1024
K = 256
ROUNDS = 2
NB = W // B
LANES = 128
CHUNKS = B // LANES

mix_weight = 0.2
step_gamma = 0.5
decode_scale = 1.0 / K

GROUPS = ((0, 2), (2, 5))
EDGE = 8
NEXT_ROW, PREV_ROW, NEXT_COL, PREV_COL = range(4)

f32 = jnp.float32
bf16 = jnp.bfloat16


def plus_minus(value, bits):
    shift = bits
    while shift > 1:
        shift = (shift + 1) // 2
        value = value ^ (value >> shift)
    return (1 - 2 * (value & 1)).astype(f32)


def rows_of(order, count):
    return plus_minus(order & lax.broadcasted_iota(jnp.int32, (count, K), 0), 4)


def low_matrix(order):
    outer, inner = rows_of((order >> 3) & 15, 16), rows_of(order & 7, 8)
    return jnp.concatenate([outer[i:i + 1] * inner for i in range(16)], axis=0).astype(bf16)


def high_signs(order, rows):
    chunk = rows_of(order >> 7, CHUNKS)
    return jnp.concatenate([jnp.broadcast_to(chunk[i:i + 1], (rows, K)) for i in range(CHUNKS)], axis=0)


def halves(value):
    top = value.astype(bf16)
    return top, (value - top.astype(f32)).astype(bf16)


def encode(diff, low, high):
    rows = diff.shape[0]
    stacked = jnp.concatenate([diff[:, c * LANES:(c + 1) * LANES] for c in range(CHUNKS)], axis=0)
    both = jnp.concatenate(halves(stacked), axis=1)
    twice = jnp.concatenate([low, low], axis=0)
    parts = high * jnp.dot(both, twice, preferred_element_type=f32)
    return jnp.sum(parts.reshape(CHUNKS, rows, K), axis=0)


def decode(code, low, high):
    rows = code.shape[0]
    spread = high * jnp.concatenate([code] * CHUNKS, axis=0)
    both = jnp.concatenate(halves(spread), axis=0)
    result = lax.dot_general(both, low, (((1,), (1,)), ((), ())), preferred_element_type=f32)
    result = result[:CHUNKS * rows] + result[CHUNKS * rows:]
    return jnp.concatenate([result[c * rows:(c + 1) * rows] for c in range(CHUNKS)], axis=1)


def kernel(n_row, n_col, x_in, h_in, s_in, order_in, bits_in, x_v, h_v, s_v,
           order_v, bits_v, sign_v, low_v, high_v, code_v, got_v,
           self_v, base_v, rows_v, cols_v, next_v, last_v, side_v, both_v, full_v,
           in_sem, send_sem, recv_sem):
    rows = x_v.shape[0]
    row, col = lax.axis_index("row"), lax.axis_index("col")
    neighbours = (
        {"row": lax.rem(row + 1, n_row)},
        {"row": lax.rem(row + n_row - 1, n_row)},
        {"col": lax.rem(col + 1, n_col)},
        {"col": lax.rem(col + n_col - 1, n_col)},
    )

    def load(i, source, target):
        return pltpu.make_async_copy(source, target, in_sem.at[i])

    order_load = load(0, order_in.at[:, :, pl.ds(0, K)], order_v)
    bits_load = load(1, bits_in, bits_v)
    x_loads = [load(2 + j, x_in.at[0, 0, :, pl.ds(j * B, B)], x_v.at[:, pl.ds(j * B, B)]) for j in range(NB)]
    h_loads = [load(2 + NB + j, h_in.at[0, 0, :, pl.ds(j * B, B)], h_v.at[:, pl.ds(j * B, B)]) for j in range(NB)]
    s_load = load(2 + 2 * NB, s_in.at[0, 0], s_v)
    edge = lax.rem(row, EDGE) == 0
    inner = jnp.logical_not(edge)
    before_edge = lax.rem(row, EDGE) == EDGE - 1
    even = lax.rem(col, 2) == 0
    odd = jnp.logical_not(even)
    early = jnp.where(edge, PREV_ROW, NEXT_ROW)
    late = jnp.where(edge, NEXT_ROW, PREV_ROW)

    barrier = pltpu.get_barrier_semaphore()

    def greet(n):
        pl.semaphore_signal(barrier, inc=1, device_id=neighbours[n], device_id_type=pl.DeviceIdType.MESH)

    greet(NEXT_COL)
    greet(PREV_COL)
    greet(PREV_ROW)
    pl.when(jnp.logical_not(before_edge))(lambda: greet(NEXT_ROW))
    for each in [order_load, bits_load] + [load for pair in zip(x_loads, h_loads) for load in pair] + [s_load]:
        each.start()

    def build(r):
        for j in range(NB):
            order = order_v[j, r:r + 1, :]
            low_v[r, j] = low_matrix(order)
            high_v[r, j] = high_signs(order, rows)

    def columns(j):
        return slice(j * B, (j + 1) * B)

    def signs(r):
        return jnp.broadcast_to((2 * bits_v[r:r + 1, :] - 1).astype(f32), (rows, W))

    def copy(r, n, g, source):
        first, last = GROUPS[g]
        part = pl.ds(first, last - first)
        return pltpu.make_async_remote_copy(
            src_ref=source.at[part],
            dst_ref=got_v.at[r, n, part],
            send_sem=send_sem.at[r, n, g],
            recv_sem=recv_sem.at[r, n, g],
            device_id=neighbours[n],
            device_id_type=pl.DeviceIdType.MESH,
        )

    def send(r, targets, g, source):
        for n in targets:
            copy(r, n, g, source).start()

    def receive(r, sources, g):
        first, last = GROUPS[g]
        for n in sources:
            arrived = got_v.at[r, n, pl.ds(first, last - first)]
            pltpu.make_async_copy(arrived, arrived, recv_sem.at[r, n, g]).wait()

    order_load.wait()
    build(0)
    bits_load.wait()
    sign_v[0] = signs(0)
    for g, (first, last) in enumerate(GROUPS):
        for j in range(first, last):
            x_loads[j].wait()
            h_loads[j].wait()
        for j in range(first, last):
            cols = columns(j)
            code_v[0, j] = encode(sign_v[0, :, cols] * (x_v[:, cols] - h_v[:, cols]), low_v[0, j], high_v[0, j])
        if g == 0:
            pl.semaphore_wait(barrier, jnp.where(edge, 3, 4))
        send(0, (NEXT_COL, PREV_COL, NEXT_ROW), g, code_v.at[0])
        pl.when(inner)(lambda g=g: send(0, (PREV_ROW,), g, code_v.at[0]))

    build(1)
    sign_v[1] = signs(1)
    sign_v[2] = step_gamma * sign_v[0] * sign_v[1]
    s_load.wait()
    for j in range(NB):
        cols = columns(j)
        decoded = decode(decode_scale * code_v[0, j], low_v[0, j], high_v[0, j])
        update = sign_v[0, :, cols] * decoded
        public = h_v[:, cols] + update
        mixed = s_v[:, cols]
        x_v[:, cols] = x_v[:, cols] - step_gamma * public
        base = x_v[:, cols] + step_gamma * mixed - public
        h_v[:, cols] = public
        s_v[:, cols] = mixed + mix_weight * update
        self_v[j] = encode(mix_weight * sign_v[2, :, cols] * decoded, low_v[1, j], high_v[1, j])
        base_v[j] = encode(sign_v[1, :, cols] * base, low_v[1, j], high_v[1, j]) + self_v[j]

    twice = jnp.where(even, 0.0, 2.0)

    def part(j, code):
        cols = columns(j)
        decoded = decode((mix_weight * decode_scale) * code, low_v[0, j], high_v[0, j])
        s_v[:, cols] = s_v[:, cols] + sign_v[0, :, cols] * decoded
        return encode(sign_v[2, :, cols] * decoded, low_v[1, j], high_v[1, j])

    for g in range(len(GROUPS)):
        receive(0, (early,), g)
    for j in range(NB):
        rows_v[j] = part(j, got_v[0, early, j])
        next_v[j] = base_v[j] + rows_v[j]

    @pl.when(jnp.logical_and(inner, even))
    def _():
        for g in range(len(GROUPS)):
            send(1, (NEXT_ROW,), g, next_v)

    for g, (first, last) in enumerate(GROUPS):
        receive(0, (NEXT_COL, PREV_COL), g)
        for j in range(first, last):
            cols_v[j] = part(j, got_v[0, NEXT_COL, j] + got_v[0, PREV_COL, j])
            last_v[j] = base_v[j] + rows_v[j] + twice * cols_v[j]
            side_v[j] = base_v[j] + cols_v[j]
        pl.when(jnp.logical_and(inner, odd))(lambda g=g: send(1, (NEXT_ROW,), g, last_v))
        pl.when(even)(lambda g=g: send(1, (NEXT_COL, PREV_COL), g, side_v))

    for g, (first, last) in enumerate(GROUPS):
        receive(0, (late,), g)
        for j in range(first, last):
            late_part = part(j, got_v[0, late, j])
            rows_v[j] = rows_v[j] + late_part
            code_v[1, j] = last_v[j] + late_part
            both_v[j] = side_v[j] + twice * rows_v[j]
        pl.when(odd)(lambda g=g: send(1, (NEXT_COL, PREV_COL), g, both_v))
        pl.when(edge)(lambda g=g: send(1, (NEXT_ROW,), g, code_v.at[1]))
        send(1, (PREV_ROW,), g, code_v.at[1])
        pl.when(edge)(lambda g=g: send(0, (PREV_ROW,), g, code_v.at[0]))

    for j in range(NB):
        cols = columns(j)
        own = base_v[j] + rows_v[j] + cols_v[j]
        full_v[j] = own
        public = h_v[:, cols] + sign_v[1, :, cols] * decode(decode_scale * own, low_v[1, j], high_v[1, j])
        h_v[:, cols] = public
        x_v[:, cols] = x_v[:, cols] + step_gamma * (2 * s_v[:, cols] - public)

    left_out = jnp.where(lax.rem(row, EDGE) == 1, 0.0, 1.0)
    for g, (first, last) in enumerate(GROUPS):
        receive(1, range(4), g)
        for j in range(first, last):
            cols = columns(j)
            total = full_v[j] + left_out * self_v[j]
            for n in range(4):
                total = total + got_v[1, n, j]
            decoded = decode((mix_weight * decode_scale) * total, low_v[1, j], high_v[1, j])
            update = sign_v[1, :, cols] * decoded
            s_v[:, cols] = s_v[:, cols] + update
            x_v[:, cols] = x_v[:, cols] + step_gamma * update
    for r in range(ROUNDS):
        for n in range(4):
            for g in range(len(GROUPS)):
                copy(r, n, g, code_v.at[r]).wait_send()


def store_kernel(x_in, h_in, s_in, x_out, h_out, s_out, sem):
    pairs = ((x_in, x_out), (h_in, h_out), (s_in, s_out))
    copies = [pltpu.make_async_copy(a, b.at[0, 0], sem.at[i]) for i, (a, b) in enumerate(pairs)]
    for copy in copies:
        copy.start()
    for copy in copies:
        copy.wait()


def local(n_row, n_col, params, public_copy, neighbour_mix, row_orders, sign_bits):
    rows = params.shape[2]
    hbm = pl.BlockSpec(memory_space=pltpu.HBM)
    vmem = pl.BlockSpec(memory_space=pltpu.VMEM)
    shape = jax.ShapeDtypeStruct(params.shape, f32)
    flat = pltpu.VMEM((rows, W), f32)
    results = pl.pallas_call(
        functools.partial(kernel, n_row, n_col),
        out_shape=(flat, flat, flat),
        in_specs=[hbm] * 5,
        out_specs=(vmem, vmem, vmem),
        scratch_shapes=[
            pltpu.VMEM((NB, ROUNDS, K), jnp.int32),
            pltpu.VMEM((ROUNDS, W), jnp.int32),
            pltpu.VMEM((3, rows, W), f32),
            pltpu.VMEM((ROUNDS, NB, LANES, K), bf16),
            pltpu.VMEM((ROUNDS, NB, CHUNKS * rows, K), f32),
            pltpu.VMEM((ROUNDS, NB, rows, K), f32),
            pltpu.VMEM((ROUNDS, 4, NB, rows, K), f32),
        ] + [pltpu.VMEM((NB, rows, K), f32)] * 9 + [
            pltpu.SemaphoreType.DMA((3 + 2 * NB,)),
            pltpu.SemaphoreType.DMA((ROUNDS, 4, len(GROUPS))),
            pltpu.SemaphoreType.DMA((ROUNDS, 4, len(GROUPS))),
        ],
        compiler_params=pltpu.CompilerParams(
            collective_id=0, has_side_effects=True, vmem_limit_bytes=32 * 1024 * 1024
        ),
    )(*(pltpu.with_memory_space_constraint(a, pltpu.HBM) for a in (
        params, public_copy, neighbour_mix, jnp.transpose(row_orders, (1, 0, 2)), sign_bits)))
    return pl.pallas_call(
        store_kernel,
        out_shape=(shape, shape, shape),
        in_specs=[vmem] * 3,
        out_specs=(hbm, hbm, hbm),
        scratch_shapes=[pltpu.SemaphoreType.DMA((3,))],
    )(*(pltpu.with_memory_space_constraint(a, pltpu.VMEM) for a in results))


def solution(mesh):
    split = P("row", "col", "shard", None)
    return jax.shard_map(
        functools.partial(local, mesh.shape["row"], mesh.shape["col"]),
        mesh=mesh,
        in_specs=(split, split, split, P(), P()),
        out_specs=(split, split, split),
        check_vma=False,
    )
```

time: 21.9 us -> 21.7 us (level)
    pallas_call x1, Pallas kernels: 20.3 us -> 20.1 us  [local(): pl.pallas_call(functools.partial(kernel, n_row, n_col), out_shape=(flat,...]
where the time goes in v5:
time: 21.7 us; the launch traced here: 21.5 us
  Pallas kernels  20.9 us (96%)
  between operations  0.64 us (3%)
    pallas_call x1, Pallas kernels, local(): pl.pallas_call(functools.partial(kernel, n_row, n_col), out_shape=(flat,...  20.1 us
    pallas_call x1, Pallas kernels, local(): pl.pallas_call(store_kernel, out_shape=(shape, shape, shape), in_specs=[v...  0.8 us

profile of v5, /device:TPU:25, one launch (start us, length us, event | category | flops | bytes accessed | tf_op | source)
XLA Modules:
  0.0 21.5 jit_solution(912093610320510509)
XLA Ops:
  0.6 20.1 %shard_map.76 = (f32[8,5120]{1,0:T(8,128)S(1)}, f32[8,5120]{1,0:T(8,128)S(1)}, f32[8,5120]{1,0:T(8,128)S(1)}) custom-call(f32[1,1,8,5120]{3,2,1,0:T(8,128)} %x_in.1, f32[1,1,8,5120]{3,2,1,0:T(8,128)} %h_in.1, f32[1,1,8,5120]{3,2,1,0:T(8,128)} %s_in.1, s32[5,2,1024]{2,1,0:T(2,128)} %bitcast.1, s32[2,5120]{1,0:T(2,128)} %bits_in.1), custom_call_target="tpu_custom_call" | custom-call | tf_op jit(solution)/shard_map/pallas_call | solution.py:264
  20.7 0.8 %shard_map.77 = (f32[1,1,8,5120]{3,2,1,0:T(8,128)}, f32[1,1,8,5120]{3,2,1,0:T(8,128)}, f32[1,1,8,5120]{3,2,1,0:T(8,128)}) custom-call(f32[8,5120]{1,0:T(8,128)S(1)} %get-tuple-element.6.x_in, f32[8,5120]{1,0:T(8,128)S(1)} %get-tuple-element.7.h_in, f32[8,5120]{1,0:T(8,128)S(1)} %get-tuple-element.8.s_in), custom_call_target="tpu_custom_call" | custom-call | tf_op jit(solution)/shard_map/pallas_call | solution.py:287

commit v6 on v5

--- a/solution.py
+++ b/solution.py
@@ -21,7 +21,7 @@
 
 GROUPS = ((0, 2), (2, 5))
 EDGE = 8
-NEXT_ROW, PREV_ROW, NEXT_COL, PREV_COL = range(4)
+NEXT_ROW, PREV_ROW, CHIP, SIDE = range(4)
 
 f32 = jnp.float32
 bf16 = jnp.bfloat16
@@ -75,15 +75,16 @@
 def kernel(n_row, n_col, x_in, h_in, s_in, order_in, bits_in, x_v, h_v, s_v,
            order_v, bits_v, sign_v, low_v, high_v, code_v, got_v,
            self_v, base_v, rows_v, cols_v, next_v, last_v, side_v, both_v, full_v,
-           in_sem, send_sem, recv_sem):
+           more_v, out_v, aside_v, back_v,
+           in_sem, send_sem, recv_sem, aside_sem, ready):
     rows = x_v.shape[0]
     row, col = lax.axis_index("row"), lax.axis_index("col")
-    neighbours = (
-        {"row": lax.rem(row + 1, n_row)},
-        {"row": lax.rem(row + n_row - 1, n_row)},
-        {"col": lax.rem(col + 1, n_col)},
-        {"col": lax.rem(col + n_col - 1, n_col)},
-    )
+    even = lax.rem(col, 2) == 0
+    odd = jnp.logical_not(even)
+    chip_col = jnp.where(even, col + 1, col - 1)
+    side_col = lax.rem(jnp.where(even, col + n_col - 1, col + 1), n_col)
+    next_row, prev_row = lax.rem(row + 1, n_row), lax.rem(row + n_row - 1, n_row)
+    neighbours = ({"row": next_row}, {"row": prev_row}, {"col": chip_col}, {"col": side_col})
 
     def load(i, source, target):
         return pltpu.make_async_copy(source, target, in_sem.at[i])
@@ -96,20 +97,44 @@
     edge = lax.rem(row, EDGE) == 0
     inner = jnp.logical_not(edge)
     before_edge = lax.rem(row, EDGE) == EDGE - 1
-    even = lax.rem(col, 2) == 0
-    odd = jnp.logical_not(even)
     early = jnp.where(edge, PREV_ROW, NEXT_ROW)
     late = jnp.where(edge, NEXT_ROW, PREV_ROW)
+    pair = jnp.where(even, side_col, col) // 2
+    middle = n_col // 4
+    lopsided = jnp.logical_or(pair < middle, pair == n_col // 2 - 1)
+    first_side = jnp.logical_and(lopsided, (pair < middle) == odd)
+    last_side = jnp.logical_not(first_side)
+    at_cut = jnp.logical_or(pair < middle, pair == n_col // 2 - 1)
+    two_before = lax.rem(row, EDGE) == EDGE - 2
+    aside_from = jnp.logical_and(even, jnp.logical_or(two_before, jnp.logical_and(before_edge, at_cut)))
+    aside_by = jnp.logical_and(before_edge, jnp.logical_and(odd, at_cut))
+    aside_to = jnp.logical_and(edge, jnp.logical_or(even, at_cut))
+    at_end = pair == n_col // 2 - 1
+    back_from = jnp.logical_and(before_edge, jnp.logical_and(odd, at_end))
+    back_by = jnp.logical_and(edge, jnp.logical_and(odd, at_end))
+    back_to = jnp.logical_and(edge, jnp.logical_and(even, at_end))
+    aside_target = {
+        "row": jnp.where(before_edge, next_row, lax.rem(row + 2, n_row)),
+        "col": jnp.where(before_edge, side_col, col),
+    }
+    aside_source = {
+        "row": jnp.where(odd, prev_row, lax.rem(row + n_row - 2, n_row)),
+        "col": jnp.where(odd, side_col, col),
+    }
 
     barrier = pltpu.get_barrier_semaphore()
 
-    def greet(n):
-        pl.semaphore_signal(barrier, inc=1, device_id=neighbours[n], device_id_type=pl.DeviceIdType.MESH)
-
-    greet(NEXT_COL)
-    greet(PREV_COL)
-    greet(PREV_ROW)
-    pl.when(jnp.logical_not(before_edge))(lambda: greet(NEXT_ROW))
+    def greet(device):
+        pl.semaphore_signal(barrier, inc=1, device_id=device, device_id_type=pl.DeviceIdType.MESH)
+
+    pl.when(jnp.logical_or(first_side, jnp.logical_not(lopsided)))(lambda: greet(neighbours[SIDE]))
+    greet(neighbours[CHIP])
+    greet(neighbours[PREV_ROW])
+    pl.when(jnp.logical_not(before_edge))(lambda: greet(neighbours[NEXT_ROW]))
+    pl.when(aside_to)(lambda: greet(aside_source))
+    pl.when(back_to)(lambda: greet({"row": prev_row, "col": side_col}))
+    greetings = 1 + jnp.where(edge, 1, 2) + jnp.where(first_side, 0, 1) + jnp.where(jnp.logical_or(aside_from, back_from), 1, 0)
+
     for each in [order_load, bits_load] + [load for pair in zip(x_loads, h_loads) for load in pair] + [s_load]:
         each.start()
 
@@ -141,11 +166,42 @@
         for n in targets:
             copy(r, n, g, source).start()
 
+    def copy_aside(g):
+        first, last = GROUPS[g]
+        part = pl.ds(first, last - first)
+        return pltpu.make_async_remote_copy(
+            src_ref=code_v.at[0, part],
+            dst_ref=aside_v.at[part],
+            send_sem=aside_sem.at[0, g],
+            recv_sem=aside_sem.at[1, g],
+            device_id=aside_target,
+            device_id_type=pl.DeviceIdType.MESH,
+        )
+
+    def copy_back(g):
+        first, last = GROUPS[g]
+        part = pl.ds(first, last - first)
+        return pltpu.make_async_remote_copy(
+            src_ref=code_v.at[0, part],
+            dst_ref=back_v.at[part],
+            send_sem=aside_sem.at[2, g],
+            recv_sem=aside_sem.at[3, g],
+            device_id={"row": next_row, "col": side_col},
+            device_id_type=pl.DeviceIdType.MESH,
+        )
+
     def receive(r, sources, g):
         first, last = GROUPS[g]
         for n in sources:
             arrived = got_v.at[r, n, pl.ds(first, last - first)]
             pltpu.make_async_copy(arrived, arrived, recv_sem.at[r, n, g]).wait()
+
+    signals = jnp.logical_and(lopsided, last_side)
+
+    @pl.when(signals)
+    def _():
+        pl.semaphore_wait(barrier, greetings)
+        pl.semaphore_signal(ready, inc=1, device_id=neighbours[SIDE], device_id_type=pl.DeviceIdType.MESH)
 
     order_load.wait()
     build(0)
@@ -159,13 +215,17 @@
             cols = columns(j)
             code_v[0, j] = encode(sign_v[0, :, cols] * (x_v[:, cols] - h_v[:, cols]), low_v[0, j], high_v[0, j])
         if g == 0:
-            pl.semaphore_wait(barrier, jnp.where(edge, 3, 4))
-        send(0, (NEXT_COL, PREV_COL, NEXT_ROW), g, code_v.at[0])
+            pl.when(jnp.logical_not(signals))(lambda: pl.semaphore_wait(barrier, greetings))
+        pl.when(last_side)(lambda g=g: send(0, (SIDE,), g, code_v.at[0]))
+        pl.when(aside_from)(lambda g=g: copy_aside(g).start())
+        pl.when(back_from)(lambda g=g: copy_back(g).start())
+        send(0, (CHIP, NEXT_ROW), g, code_v.at[0])
         pl.when(inner)(lambda g=g: send(0, (PREV_ROW,), g, code_v.at[0]))
 
     build(1)
     sign_v[1] = signs(1)
     sign_v[2] = step_gamma * sign_v[0] * sign_v[1]
+    left_out = jnp.where(lax.rem(row, EDGE) == 1, 0.0, 1.0)
     s_load.wait()
     for j in range(NB):
         cols = columns(j)
@@ -178,35 +238,58 @@
         h_v[:, cols] = public
         s_v[:, cols] = mixed + mix_weight * update
         self_v[j] = encode(mix_weight * sign_v[2, :, cols] * decoded, low_v[1, j], high_v[1, j])
+        more_v[j] = left_out * self_v[j]
         base_v[j] = encode(sign_v[1, :, cols] * base, low_v[1, j], high_v[1, j]) + self_v[j]
 
     twice = jnp.where(even, 0.0, 2.0)
 
-    def part(j, code):
+    def part(j, code, mix=True):
         cols = columns(j)
         decoded = decode((mix_weight * decode_scale) * code, low_v[0, j], high_v[0, j])
-        s_v[:, cols] = s_v[:, cols] + sign_v[0, :, cols] * decoded
+        if mix:
+            s_v[:, cols] = s_v[:, cols] + sign_v[0, :, cols] * decoded
         return encode(sign_v[2, :, cols] * decoded, low_v[1, j], high_v[1, j])
+
+    @pl.when(jnp.logical_and(before_edge, even))
+    def _():
+        for g in range(len(GROUPS)):
+            send(1, (NEXT_ROW,), g, base_v)
+
+    for g in range(len(GROUPS)):
+        receive(0, (CHIP,), g)
+    for j in range(NB):
+        cols_v[j] = part(j, got_v[0, CHIP, j])
+
+    @pl.when(first_side)
+    def _():
+        pl.semaphore_wait(ready, 1)
+        for g in range(len(GROUPS)):
+            send(0, (SIDE,), g, code_v.at[0])
 
     for g in range(len(GROUPS)):
         receive(0, (early,), g)
     for j in range(NB):
         rows_v[j] = part(j, got_v[0, early, j])
-        next_v[j] = base_v[j] + rows_v[j]
-
-    @pl.when(jnp.logical_and(inner, even))
+        next_v[j] = base_v[j] + rows_v[j] + twice * cols_v[j]
+
+    @pl.when(jnp.logical_or(jnp.logical_and(jnp.logical_and(inner, even), jnp.logical_not(before_edge)), aside_by))
     def _():
         for g in range(len(GROUPS)):
             send(1, (NEXT_ROW,), g, next_v)
 
     for g, (first, last) in enumerate(GROUPS):
-        receive(0, (NEXT_COL, PREV_COL), g)
+        receive(0, (SIDE,), g)
         for j in range(first, last):
-            cols_v[j] = part(j, got_v[0, NEXT_COL, j] + got_v[0, PREV_COL, j])
-            last_v[j] = base_v[j] + rows_v[j] + twice * cols_v[j]
+            side_part = part(j, got_v[0, SIDE, j])
+            last_v[j] = next_v[j] + twice * side_part
+            cols_v[j] = cols_v[j] + side_part
             side_v[j] = base_v[j] + cols_v[j]
-        pl.when(jnp.logical_and(inner, odd))(lambda g=g: send(1, (NEXT_ROW,), g, last_v))
-        pl.when(even)(lambda g=g: send(1, (NEXT_COL, PREV_COL), g, side_v))
+            both_v[j] = side_v[j] + twice * rows_v[j]
+        pl.when(jnp.logical_and(jnp.logical_and(inner, odd), jnp.logical_not(aside_by)))(
+            lambda g=g: send(1, (NEXT_ROW,), g, last_v)
+        )
+        pl.when(even)(lambda g=g: send(1, (CHIP, SIDE), g, side_v))
+        pl.when(back_by)(lambda g=g: send(1, (SIDE,), g, both_v))
 
     for g, (first, last) in enumerate(GROUPS):
         receive(0, (late,), g)
@@ -214,8 +297,9 @@
             late_part = part(j, got_v[0, late, j])
             rows_v[j] = rows_v[j] + late_part
             code_v[1, j] = last_v[j] + late_part
-            both_v[j] = side_v[j] + twice * rows_v[j]
-        pl.when(odd)(lambda g=g: send(1, (NEXT_COL, PREV_COL), g, both_v))
+            out_v[j] = side_v[j] + twice * rows_v[j]
+        pl.when(jnp.logical_and(odd, jnp.logical_not(back_by)))(lambda g=g: send(1, (SIDE,), g, out_v))
+        pl.when(odd)(lambda g=g: send(1, (CHIP,), g, out_v))
         pl.when(edge)(lambda g=g: send(1, (NEXT_ROW,), g, code_v.at[1]))
         send(1, (PREV_ROW,), g, code_v.at[1])
         pl.when(edge)(lambda g=g: send(0, (PREV_ROW,), g, code_v.at[0]))
@@ -228,12 +312,25 @@
         h_v[:, cols] = public
         x_v[:, cols] = x_v[:, cols] + step_gamma * (2 * s_v[:, cols] - public)
 
-    left_out = jnp.where(lax.rem(row, EDGE) == 1, 0.0, 1.0)
+    @pl.when(aside_to)
+    def _():
+        for g in range(len(GROUPS)):
+            copy_aside(g).wait_recv()
+        for j in range(NB):
+            more_v[j] = more_v[j] + jnp.where(odd, 2.0, 1.0) * part(j, aside_v[j], mix=False)
+
+    @pl.when(back_to)
+    def _():
+        for g in range(len(GROUPS)):
+            copy_back(g).wait_recv()
+        for j in range(NB):
+            more_v[j] = more_v[j] + 2 * part(j, back_v[j], mix=False)
+
     for g, (first, last) in enumerate(GROUPS):
         receive(1, range(4), g)
         for j in range(first, last):
             cols = columns(j)
-            total = full_v[j] + left_out * self_v[j]
+            total = full_v[j] + more_v[j]
             for n in range(4):
                 total = total + got_v[1, n, j]
             decoded = decode((mix_weight * decode_scale) * total, low_v[1, j], high_v[1, j])
@@ -244,6 +341,16 @@
         for n in range(4):
             for g in range(len(GROUPS)):
                 copy(r, n, g, code_v.at[r]).wait_send()
+
+    @pl.when(aside_from)
+    def _():
+        for g in range(len(GROUPS)):
+            copy_aside(g).wait_send()
+
+    @pl.when(back_from)
+    def _():
+        for g in range(len(GROUPS)):
+            copy_back(g).wait_send()
 
 
 def store_kernel(x_in, h_in, s_in, x_out, h_out, s_out, sem):
@@ -274,10 +381,12 @@
             pltpu.VMEM((ROUNDS, NB, CHUNKS * rows, K), f32),
             pltpu.VMEM((ROUNDS, NB, rows, K), f32),
             pltpu.VMEM((ROUNDS, 4, NB, rows, K), f32),
-        ] + [pltpu.VMEM((NB, rows, K), f32)] * 9 + [
+        ] + [pltpu.VMEM((NB, rows, K), f32)] * 13 + [
             pltpu.SemaphoreType.DMA((3 + 2 * NB,)),
             pltpu.SemaphoreType.DMA((ROUNDS, 4, len(GROUPS))),
             pltpu.SemaphoreType.DMA((ROUNDS, 4, len(GROUPS))),
+            pltpu.SemaphoreType.DMA((4, len(GROUPS))),
+            pltpu.SemaphoreType.REGULAR,
         ],
         compiler_params=pltpu.CompilerParams(
             collective_id=0, has_side_effects=True, vmem_limit_bytes=32 * 1024 * 1024

time: 21.7 us -> 21.2 us (0.977)
  the two profiles are of different devices: /device:TPU:25 before, /device:TPU:1 now
where the time goes in v6:
time: 21.2 us; the launch traced here: 21.1 us
  Pallas kernels  20.5 us (97%)
  between operations  0.64 us (3%)
    pallas_call x1, Pallas kernels, local(): pl.pallas_call(functools.partial(kernel, n_row, n_col), out_shape=(flat,...  19.7 us
    pallas_call x1, Pallas kernels, local(): pl.pallas_call(store_kernel, out_shape=(shape, shape, shape), in_specs=[v...  0.8 us

profile of v6, /device:TPU:1, one launch (start us, length us, event | category | flops | bytes accessed | tf_op | source)
XLA Modules:
  0.0 21.1 jit_solution(8036347407440431604)
XLA Ops:
  0.6 19.7 %shard_map.76 = (f32[8,5120]{1,0:T(8,128)S(1)}, f32[8,5120]{1,0:T(8,128)S(1)}, f32[8,5120]{1,0:T(8,128)S(1)}) custom-call(f32[1,1,8,5120]{3,2,1,0:T(8,128)} %x_in.1, f32[1,1,8,5120]{3,2,1,0:T(8,128)} %h_in.1, f32[1,1,8,5120]{3,2,1,0:T(8,128)} %s_in.1, s32[5,2,1024]{2,1,0:T(2,128)} %bitcast.1, s32[2,5120]{1,0:T(2,128)} %bits_in.1), custom_call_target="tpu_custom_call" | custom-call | tf_op jit(solution)/shard_map/pallas_call | solution.py:371
  20.3 0.8 %shard_map.77 = (f32[1,1,8,5120]{3,2,1,0:T(8,128)}, f32[1,1,8,5120]{3,2,1,0:T(8,128)}, f32[1,1,8,5120]{3,2,1,0:T(8,128)}) custom-call(f32[8,5120]{1,0:T(8,128)S(1)} %get-tuple-element.6.x_in, f32[8,5120]{1,0:T(8,128)S(1)} %get-tuple-element.7.h_in, f32[8,5120]{1,0:T(8,128)S(1)} %get-tuple-element.8.s_in), custom_call_target="tpu_custom_call" | custom-call | tf_op jit(solution)/shard_map/pallas_call | solution.py:396

commit v7 on v6

--- a/solution.py
+++ b/solution.py
@@ -72,8 +72,8 @@
     return jnp.concatenate([result[c * rows:(c + 1) * rows] for c in range(CHUNKS)], axis=1)
 
 
-def kernel(n_row, n_col, x_in, h_in, s_in, order_in, bits_in, x_v, h_v, s_v,
-           order_v, bits_v, sign_v, low_v, high_v, code_v, got_v,
+def kernel(n_row, n_col, x_in, h_in, s_in, order_in, bits_in, x_v, h_v, s_v, total_v, low1_v, high1_v, sign1_v,
+           order_v, bits_v, sign0_v, low0_v, high0_v, code_v, got_v,
            self_v, base_v, rows_v, cols_v, next_v, last_v, side_v, both_v, full_v,
            more_v, out_v, aside_v, back_v,
            in_sem, send_sem, recv_sem, aside_sem, ready):
@@ -138,11 +138,13 @@
     for each in [order_load, bits_load] + [load for pair in zip(x_loads, h_loads) for load in pair] + [s_load]:
         each.start()
 
+    low_v, high_v = (low0_v, low1_v), (high0_v, high1_v)
+
     def build(r):
         for j in range(NB):
             order = order_v[j, r:r + 1, :]
-            low_v[r, j] = low_matrix(order)
-            high_v[r, j] = high_signs(order, rows)
+            low_v[r][j] = low_matrix(order)
+            high_v[r][j] = high_signs(order, rows)
 
     def columns(j):
         return slice(j * B, (j + 1) * B)
@@ -206,49 +208,49 @@
     order_load.wait()
     build(0)
     bits_load.wait()
-    sign_v[0] = signs(0)
+    sign0_v[0] = signs(0)
     for g, (first, last) in enumerate(GROUPS):
         for j in range(first, last):
             x_loads[j].wait()
             h_loads[j].wait()
         for j in range(first, last):
             cols = columns(j)
-            code_v[0, j] = encode(sign_v[0, :, cols] * (x_v[:, cols] - h_v[:, cols]), low_v[0, j], high_v[0, j])
+            code_v[0, j] = encode(sign0_v[0, :, cols] * (x_v[:, cols] - h_v[:, cols]), low0_v[j], high0_v[j])
         if g == 0:
             pl.when(jnp.logical_not(signals))(lambda: pl.semaphore_wait(barrier, greetings))
+        pl.when(aside_from)(lambda g=g: copy_aside(g).start())
         pl.when(last_side)(lambda g=g: send(0, (SIDE,), g, code_v.at[0]))
-        pl.when(aside_from)(lambda g=g: copy_aside(g).start())
         pl.when(back_from)(lambda g=g: copy_back(g).start())
         send(0, (CHIP, NEXT_ROW), g, code_v.at[0])
         pl.when(inner)(lambda g=g: send(0, (PREV_ROW,), g, code_v.at[0]))
 
     build(1)
-    sign_v[1] = signs(1)
-    sign_v[2] = step_gamma * sign_v[0] * sign_v[1]
+    sign1_v[...] = signs(1)
+    sign0_v[1] = step_gamma * sign0_v[0] * sign1_v[...]
     left_out = jnp.where(lax.rem(row, EDGE) == 1, 0.0, 1.0)
     s_load.wait()
     for j in range(NB):
         cols = columns(j)
-        decoded = decode(decode_scale * code_v[0, j], low_v[0, j], high_v[0, j])
-        update = sign_v[0, :, cols] * decoded
+        decoded = decode(decode_scale * code_v[0, j], low0_v[j], high0_v[j])
+        update = sign0_v[0, :, cols] * decoded
         public = h_v[:, cols] + update
         mixed = s_v[:, cols]
         x_v[:, cols] = x_v[:, cols] - step_gamma * public
         base = x_v[:, cols] + step_gamma * mixed - public
         h_v[:, cols] = public
         s_v[:, cols] = mixed + mix_weight * update
-        self_v[j] = encode(mix_weight * sign_v[2, :, cols] * decoded, low_v[1, j], high_v[1, j])
+        self_v[j] = encode(mix_weight * sign0_v[1, :, cols] * decoded, low1_v[j], high1_v[j])
         more_v[j] = left_out * self_v[j]
-        base_v[j] = encode(sign_v[1, :, cols] * base, low_v[1, j], high_v[1, j]) + self_v[j]
+        base_v[j] = encode(sign1_v[:, cols] * base, low1_v[j], high1_v[j]) + self_v[j]
 
     twice = jnp.where(even, 0.0, 2.0)
 
     def part(j, code, mix=True):
         cols = columns(j)
-        decoded = decode((mix_weight * decode_scale) * code, low_v[0, j], high_v[0, j])
+        decoded = decode((mix_weight * decode_scale) * code, low0_v[j], high0_v[j])
         if mix:
-            s_v[:, cols] = s_v[:, cols] + sign_v[0, :, cols] * decoded
-        return encode(sign_v[2, :, cols] * decoded, low_v[1, j], high_v[1, j])
+            s_v[:, cols] = s_v[:, cols] + sign0_v[0, :, cols] * decoded
+        return encode(sign0_v[1, :, cols] * decoded, low1_v[j], high1_v[j])
 
     @pl.when(jnp.logical_and(before_edge, even))
     def _():
@@ -308,16 +310,16 @@
         cols = columns(j)
         own = base_v[j] + rows_v[j] + cols_v[j]
         full_v[j] = own
-        public = h_v[:, cols] + sign_v[1, :, cols] * decode(decode_scale * own, low_v[1, j], high_v[1, j])
+        public = h_v[:, cols] + sign1_v[:, cols] * decode(decode_scale * own, low1_v[j], high1_v[j])
         h_v[:, cols] = public
         x_v[:, cols] = x_v[:, cols] + step_gamma * (2 * s_v[:, cols] - public)
 
     @pl.when(aside_to)
     def _():
-        for g in range(len(GROUPS)):
+        for g, (first, last) in enumerate(GROUPS):
             copy_aside(g).wait_recv()
-        for j in range(NB):
-            more_v[j] = more_v[j] + jnp.where(odd, 2.0, 1.0) * part(j, aside_v[j], mix=False)
+            for j in range(first, last):
+                more_v[j] = more_v[j] + jnp.where(odd, 2.0, 1.0) * part(j, aside_v[j], mix=False)
 
     @pl.when(back_to)
     def _():
@@ -329,14 +331,10 @@
     for g, (first, last) in enumerate(GROUPS):
         receive(1, range(4), g)
         for j in range(first, last):
-            cols = columns(j)
             total = full_v[j] + more_v[j]
             for n in range(4):
                 total = total + got_v[1, n, j]
-            decoded = decode((mix_weight * decode_scale) * total, low_v[1, j], high_v[1, j])
-            update = sign_v[1, :, cols] * decoded
-            s_v[:, cols] = s_v[:, cols] + update
-            x_v[:, cols] = x_v[:, cols] + step_gamma * update
+            total_v[j] = (mix_weight * decode_scale) * total
     for r in range(ROUNDS):
         for n in range(4):
             for g in range(len(GROUPS)):
@@ -353,11 +351,17 @@
             copy_back(g).wait_send()
 
 
-def store_kernel(x_in, h_in, s_in, x_out, h_out, s_out, sem):
-    pairs = ((x_in, x_out), (h_in, h_out), (s_in, s_out))
-    copies = [pltpu.make_async_copy(a, b.at[0, 0], sem.at[i]) for i, (a, b) in enumerate(pairs)]
-    for copy in copies:
-        copy.start()
+def last_kernel(x_in, h_in, s_in, total, low, high, sign, x_out, h_out, s_out, x_v, s_v, sem):
+    copies = [pltpu.make_async_copy(h_in, h_out.at[0, 0], sem.at[0])]
+    copies[0].start()
+    for j in range(NB):
+        cols = pl.ds(j * B, B)
+        update = sign[:, cols] * decode(total[j], low[j], high[j])
+        s_v[:, cols] = s_in[:, cols] + update
+        x_v[:, cols] = x_in[:, cols] + step_gamma * update
+        for i, (source, target) in enumerate(((s_v, s_out), (x_v, x_out))):
+            copies.append(pltpu.make_async_copy(source.at[:, cols], target.at[0, 0, :, cols], sem.at[1 + 2 * j + i]))
+            copies[-1].start()
     for copy in copies:
         copy.wait()
 
@@ -368,17 +372,20 @@
     vmem = pl.BlockSpec(memory_space=pltpu.VMEM)
     shape = jax.ShapeDtypeStruct(params.shape, f32)
     flat = pltpu.VMEM((rows, W), f32)
+    total = pltpu.VMEM((NB, rows, K), f32)
+    low = pltpu.VMEM((NB, LANES, K), bf16)
+    high = pltpu.VMEM((NB, CHUNKS * rows, K), f32)
     results = pl.pallas_call(
         functools.partial(kernel, n_row, n_col),
-        out_shape=(flat, flat, flat),
+        out_shape=(flat, flat, flat, total, low, high, flat),
         in_specs=[hbm] * 5,
-        out_specs=(vmem, vmem, vmem),
+        out_specs=(vmem,) * 7,
         scratch_shapes=[
             pltpu.VMEM((NB, ROUNDS, K), jnp.int32),
             pltpu.VMEM((ROUNDS, W), jnp.int32),
-            pltpu.VMEM((3, rows, W), f32),
-            pltpu.VMEM((ROUNDS, NB, LANES, K), bf16),
-            pltpu.VMEM((ROUNDS, NB, CHUNKS * rows, K), f32),
+            pltpu.VMEM((2, rows, W), f32),
+            pltpu.VMEM((NB, LANES, K), bf16),
+            pltpu.VMEM((NB, CHUNKS * rows, K), f32),
             pltpu.VMEM((ROUNDS, NB, rows, K), f32),
             pltpu.VMEM((ROUNDS, 4, NB, rows, K), f32),
         ] + [pltpu.VMEM((NB, rows, K), f32)] * 13 + [
@@ -394,11 +401,11 @@
     )(*(pltpu.with_memory_space_constraint(a, pltpu.HBM) for a in (
         params, public_copy, neighbour_mix, jnp.transpose(row_orders, (1, 0, 2)), sign_bits)))
     return pl.pallas_call(
-        store_kernel,
+        last_kernel,
         out_shape=(shape, shape, shape),
-        in_specs=[vmem] * 3,
+        in_specs=[vmem] * 7,
         out_specs=(hbm, hbm, hbm),
-        scratch_shapes=[pltpu.SemaphoreType.DMA((3,))],
+        scratch_shapes=[pltpu.VMEM((rows, W), f32), pltpu.VMEM((rows, W), f32), pltpu.SemaphoreType.DMA((1 + 2 * NB,))],
     )(*(pltpu.with_memory_space_constraint(a, pltpu.VMEM) for a in results))
 
 

time: 21.2 us -> 21.2 us (level)
    pallas_call x1, Pallas kernels: 19.7 us -> 19.4 us  [local(): pl.pallas_call(functools.partial(kernel, n_row, n_col), out_shape=(flat,...]
    pallas_call x1, Pallas kernels: 0.8 us -> 1.02 us  [local(): pl.pallas_call(last_kernel, out_shape=(shape, shape, shape), in_specs=[vm...]
where the time goes in v7:
time: 21.2 us; the launch traced here: 21.1 us
  Pallas kernels  20.4 us (96%)
  between operations  0.64 us (3%)
    pallas_call x1, Pallas kernels, local(): pl.pallas_call(functools.partial(kernel, n_row, n_col), out_shape=(flat,...  19.4 us
    pallas_call x1, Pallas kernels, local(): pl.pallas_call(last_kernel, out_shape=(shape, shape, shape), in_specs=[vm...  1.02 us

profile of v7, /device:TPU:1, one launch (start us, length us, event | category | flops | bytes accessed | tf_op | source)
XLA Modules:
  0.0 21.1 jit_solution(7108649288983099976)
XLA Ops:
  0.6 19.4 %shard_map.76 = (f32[8,5120]{1,0:T(8,128)S(1)}, f32[8,5120]{1,0:T(8,128)S(1)}, f32[8,5120]{1,0:T(8,128)S(1)}, f32[5,8,256]{2,1,0:T(8,128)S(1)}, bf16[5,128,256]{...) custom-call(f32[1,1,8,5120]{3,2,1,0:T(8,128)} %x_in.1, f32[1,1,8,5120]{3,2,1,0:T(8,128)} %h_in.1, ...), custom_call_target="tpu_custom_call" | custom-call | tf_op jit(solution)/shard_map/pallas_call | solution.py:378
  20.1 1.0 %shard_map.77 = (f32[1,1,8,5120]{3,2,1,0:T(8,128)}, f32[1,1,8,5120]{3,2,1,0:T(8,128)}, f32[1,1,8,5120]{3,2,1,0:T(8,128)}) custom-call(f32[8,5120]{1,0:T(8,128)S(1)} %get-tuple-element.10.x_in, f32[8,5120]{1,0:T(8,128)S(1)} %get-tuple-element.11.h_in, f32[8,5120]{1,0:T(8,128)S(1)} %get-tuple-element.12.s_in, f32[5,8,256]{2,1,0:T(8,128)S(1)} %get-tuple-element.13.total, ...), custom_call_target="tpu_custom_call" | custom-call | tf_op jit(solution)/shard_map/pallas_call | solution.py:403

commit v8 on v6

--- a/solution.py
+++ b/solution.py
@@ -216,11 +216,17 @@
             code_v[0, j] = encode(sign_v[0, :, cols] * (x_v[:, cols] - h_v[:, cols]), low_v[0, j], high_v[0, j])
         if g == 0:
             pl.when(jnp.logical_not(signals))(lambda: pl.semaphore_wait(barrier, greetings))
+        pl.when(aside_from)(lambda g=g: copy_aside(g).start())
         pl.when(last_side)(lambda g=g: send(0, (SIDE,), g, code_v.at[0]))
-        pl.when(aside_from)(lambda g=g: copy_aside(g).start())
         pl.when(back_from)(lambda g=g: copy_back(g).start())
-        send(0, (CHIP, NEXT_ROW), g, code_v.at[0])
+        send(0, (CHIP,), g, code_v.at[0])
+        pl.when(jnp.logical_not(aside_from))(lambda g=g: send(0, (NEXT_ROW,), g, code_v.at[0]))
         pl.when(inner)(lambda g=g: send(0, (PREV_ROW,), g, code_v.at[0]))
+
+    @pl.when(aside_from)
+    def _():
+        for g in range(len(GROUPS)):
+            send(0, (NEXT_ROW,), g, code_v.at[0])
 
     build(1)
     sign_v[1] = signs(1)

time: 21.2 us -> 21.2 us (level)
  no operation moved by 1% of the time
where the time goes in v8:
time: 21.2 us; the launch traced here: 21.1 us
  Pallas kernels  20.4 us (96%)
  between operations  0.64 us (3%)
    pallas_call x1, Pallas kernels, local(): pl.pallas_call(functools.partial(kernel, n_row, n_col), out_shape=(flat,...  19.6 us
    pallas_call x1, Pallas kernels, local(): pl.pallas_call(store_kernel, out_shape=(shape, shape, shape), in_specs=[v...  0.8 us

profile of v8, /device:TPU:1, one launch (start us, length us, event | category | flops | bytes accessed | tf_op | source)
XLA Modules:
  0.0 21.1 jit_solution(12873214281098615819)
XLA Ops:
  0.6 19.6 %shard_map.76 = (f32[8,5120]{1,0:T(8,128)S(1)}, f32[8,5120]{1,0:T(8,128)S(1)}, f32[8,5120]{1,0:T(8,128)S(1)}) custom-call(f32[1,1,8,5120]{3,2,1,0:T(8,128)} %x_in.1, f32[1,1,8,5120]{3,2,1,0:T(8,128)} %h_in.1, f32[1,1,8,5120]{3,2,1,0:T(8,128)} %s_in.1, s32[5,2,1024]{2,1,0:T(2,128)} %bitcast.1, s32[2,5120]{1,0:T(2,128)} %bits_in.1), custom_call_target="tpu_custom_call" | custom-call | tf_op jit(solution)/shard_map/pallas_call | solution.py:377
  20.3 0.8 %shard_map.77 = (f32[1,1,8,5120]{3,2,1,0:T(8,128)}, f32[1,1,8,5120]{3,2,1,0:T(8,128)}, f32[1,1,8,5120]{3,2,1,0:T(8,128)}) custom-call(f32[8,5120]{1,0:T(8,128)S(1)} %get-tuple-element.6.x_in, f32[8,5120]{1,0:T(8,128)S(1)} %get-tuple-element.7.h_in, f32[8,5120]{1,0:T(8,128)S(1)} %get-tuple-element.8.s_in), custom_call_target="tpu_custom_call" | custom-call | tf_op jit(solution)/shard_map/pallas_call | solution.py:402
